TPU v7x, 32 devices: a whole 2x2x4 slice. The times are simulated.
32 devices in a mesh: blk: 8 (over z, x), walk: 4 (over y, core).
Axes of the slice: x: 2, y: 2, z: 4, core: 2. Of those that a mesh axis runs over, the one named last changes fastest.
Arguments:
- green_half: bfloat16 [32, 50, 200], P(('blk', 'walk')), may hold values from -6 to 6
- chol_half: bfloat16 [600, 50, 200], P('blk'), may hold values from -0.0023956299 to 0.0023956299
- one_body: float32 [50, 200], replicated, may hold values from -0.06 to 0.06
- field_noise: float32 [32, 600], P(('blk', 'walk')), may hold values from -6 to 6
- old_weight: float32 [32], P(('blk', 'walk')), may hold values from 0.5 to 2
Outputs:
- force_bias: float32 [32, 600], P(('blk', 'walk'))
- energy: float32 [32], P(('blk', 'walk'))
- new_weight: float32 [32], P(('blk', 'walk'))
- comb_offset: float32 [32], P(('blk', 'walk'))
All inputs are finite; a program needn't handle non-finite values.
Results may differ from a plain program's by a relative error of at most 0.00045.
Values may be sent and summed in bfloat16 or wider, within the bound.
No kernel may reach another device: no remote copies, remote signals or barrier semaphores. Data moves between devices by JAX's collectives and lax.ppermute only.
A program may use at most 64 MiB of HBM per device.

v0:
```python
import jax
import jax.numpy as jnp
from jax import lax
from jax.sharding import PartitionSpec as P


def block_size(walker_rows):
    best = 1
    for count in range(1, min(walker_rows, 4) + 1):
        if walker_rows % count == 0:
            best = count
    return best


def lower_sum(values, rank_here):
    ranks = jnp.arange(values.shape[0], dtype=jnp.int32)
    return jnp.sum(jnp.where(ranks < rank_here, values, jnp.float32(0.0)))


def on_device(green_half, chol_half, one_body, field_noise, old_weight):
    slab_rows = chol_half.shape[0]
    occupied = chol_half.shape[1]
    orbitals = chol_half.shape[2]
    local_walkers = green_half.shape[0]

    def crossed_of(walkers):
        table = jnp.einsum("nip,wjp->wnij", chol_half, walkers, preferred_element_type=jnp.float32)
        return jnp.einsum("wnij,wnji->wn", table, table)

    arrived = lax.all_gather(green_half, "blk", axis=0, tiled=True)
    count = arrived.shape[0]
    traces = jnp.einsum("nip,wip->wn", chol_half, arrived, preferred_element_type=jnp.float32)
    group = block_size(count)
    grouped = arrived.reshape(count // group, group, occupied, orbitals)
    crossed = lax.map(crossed_of, grouped).reshape(count, slab_rows)
    partials = jnp.stack([traces, crossed])
    returned_parts = lax.all_to_all(partials, "blk", split_axis=1, concat_axis=2, tiled=True)
    force_bias = returned_parts[0]
    crossed_total = jnp.sum(returned_parts[1], axis=1)
    kinetic = jnp.sum(green_half.astype(jnp.float32) * one_body, axis=(1, 2))
    coulomb = 0.5 * jnp.sum(force_bias * force_bias, axis=1)
    energy = kinetic + coulomb - 0.5 * crossed_total
    shifted = jnp.float32(-0.1) * force_bias
    importance = jnp.sum(field_noise * shifted + 0.5 * shifted * shifted, axis=1)
    new_weight = old_weight * jnp.exp(importance - 0.01 * energy)
    inside = jnp.cumsum(new_weight) - new_weight
    own_total = jnp.sum(new_weight)
    devices = lax.axis_size(("blk", "walk"))
    rank_here = lax.axis_index(("blk", "walk"))
    walk_totals = lax.all_gather(own_total[None], "walk", axis=0, tiled=True)
    within_group = lower_sum(walk_totals, lax.axis_index("walk"))
    group_total = jnp.sum(walk_totals)
    cycle_totals = lax.all_gather(group_total[None], "blk", axis=0, tiled=True)
    before = lower_sum(cycle_totals, lax.axis_index("blk")) + within_group
    grand_total = jnp.sum(cycle_totals)
    walker_count = local_walkers * devices
    index_of = (rank_here * local_walkers + jnp.arange(local_walkers, dtype=jnp.int32)).astype(
        jnp.float32
    )
    comb_offset = (before + inside) * walker_count / grand_total - index_of
    return (force_bias, energy, new_weight, comb_offset)


def solution(mesh):
    placed = (
        P(("blk", "walk"), None, None),
        P("blk", None, None),
        P(),
        P(("blk", "walk"), None),
        P(("blk", "walk")),
    )
    return jax.shard_map(
        on_device,
        mesh=mesh,
        in_specs=placed,
        out_specs=(
            P(("blk", "walk"), None),
            P(("blk", "walk")),
            P(("blk", "walk")),
            P(("blk", "walk")),
        ),
        check_vma=False,
    )
```

profile of v0, /device:TPU:0, one launch (start us, length us, event | category | flops | bytes accessed | tf_op | source)
XLA Modules:
  0.0 89.4 jit_solution(10704871605503071615)
XLA Ops:
  0.6 0.0 copy-start
  0.7 32.8 %all_gather.9 = bf16[8,50,200]{2,1,0:T(8,128)(2,1)S(1)} all-gather(bf16[1,50,200]{2,1,0:T(8,128)(2,1)} %param.7), channel_id=1, replica_groups=mesh['blk'=8,'walk'=4] {'blk'}, dimensions={0}, use_global_device_ids=true | all-gather | bytes 180000 | tf_op jit(solution)/shard_map/all_gather | solution.py:30
  33.5 2.2 %convolution_bitcast_fusion = f32[1,8,75]{2,1,0:T(8,128)S(1)} fusion(bf16[75,50,200]{2,0,1:T(8,128)(2,1)} %param.8, bf16[8,50,200]{2,1,0:T(8,128)(2,1)S(1)} %all_gather.9), kind=kOutput, calls=%fused_computation.8 | convolution fusion | flops 12000000 | bytes 1662400 | tf_op jit(solution)/shard_map/nip,wip->wn/dot_general | solution.py:32
  35.7 0.0 copy-done
  35.7 0.0 copy-start.1
  35.7 0.0 copy-start.2
  35.7 0.0 copy-start.6
  35.7 0.0 copy-start.5
  35.7 0.0 copy-start.4
  35.7 4.3 %while.10 = (s32[]{:T(128)}, f32[2,4,75]{2,1,0:T(4,128)S(1)}, bf16[2,4,50,200]{3,2,1,0:T(8,128)(2,1)S(1)}, bf16[75,50,200]{2,0,1:T(8,128)(2,1)S(1)}, s32[]{:T(128)}) while((s32[]{:T(128)}, f32[2,4,75]{2,1,0:T(4,128)S(1)}, bf16[2,4,50,200]{3,2,1,0:T(8,128)(2,1)S(1)}, bf16[75,50,200]{2,0,1:T(8,128)(2,1)S(1)}, s32[]{:T(128)}) %tuple.32), condition=%wide.region_1.2_spmd, body=%wide.region_0.1_spmd.sunk | while | flops 301499712 | bytes 11168053 | solution.py:35
  35.7 0.9 %fusion.19 = f32[4,50,75,50]{2,1,3,0:T(8,128)S(1)} fusion(bf16[75,50,200]{2,0,1:T(8,128)(2,1)S(1)} %get-tuple-element.86, bf16[2,4,50,200]{3,2,1,0:T(8,128)(2,1)S(1)} %get-tuple-element.85, s32[]{:T(128)} %get-tuple-element.78), kind=kOutput, calls=%fused_computation.2.clone.1 | convolution fusion | flops 300000000 | bytes 5162692 | tf_op jit(solution)/shard_map/while/body/eval_jaxpr/nip,wjp->wnij/dot_general | solution.py:27
  36.7 1.2 %fusion.20 = f32[4,75]{1,0:T(4,128)S(1)} fusion(f32[4,50,75,50]{2,1,3,0:T(8,128)S(1)} %fusion.19, f32[4,75,50,50]{1,3,2,0:T(8,128)S(1)} %bitcast.45), kind=kLoop, calls=%fused_computation.1.clone.1 | loop fusion | flops 1499700 | bytes 6001200 | tf_op jit(solution)/shard_map/while/body/eval_jaxpr/wnij,wnji->wn/dot_general | solution.py:28
  37.9 0.9 %fusion.19 = f32[4,50,75,50]{2,1,3,0:T(8,128)S(1)} fusion(bf16[75,50,200]{2,0,1:T(8,128)(2,1)S(1)} %get-tuple-element.86, bf16[2,4,50,200]{3,2,1,0:T(8,128)(2,1)S(1)} %get-tuple-element.85, s32[]{:T(128)} %get-tuple-element.78), kind=kOutput, calls=%fused_computation.2.clone.1 | convolution fusion | flops 300000000 | bytes 5162692 | tf_op jit(solution)/shard_map/while/body/eval_jaxpr/nip,wjp->wnij/dot_general | solution.py:27
  38.8 1.2 %fusion.20 = f32[4,75]{1,0:T(4,128)S(1)} fusion(f32[4,50,75,50]{2,1,3,0:T(8,128)S(1)} %fusion.19, f32[4,75,50,50]{1,3,2,0:T(8,128)S(1)} %bitcast.45), kind=kLoop, calls=%fused_computation.1.clone.1 | loop fusion | flops 1499700 | bytes 6001200 | tf_op jit(solution)/shard_map/while/body/eval_jaxpr/wnij,wnji->wn/dot_general | solution.py:28
  40.0 0.6 copy.14
  40.6 5.5 %all-to-all-start = ((f32[2,8,75]{2,0,1:T(2,128)}), f32[2,8,75]{2,0,1:T(2,128)S(1)}, u32[]{:S(2)}, u32[]{:S(2)}) async-start(f32[2,8,75]{2,0,1:T(2,128)} %copy.14), calls=%async_computation | async-start | bytes 16384 | tf_op jit(solution)/shard_map/all_to_all | solution.py:37
  46.1 0.0 copy-done.1
  46.2 0.0 copy-done.2
  46.2 0.6 fusion.7
  47.4 0.0 copy-done.6
  47.4 0.6 dynamic-slice
  48.0 0.0 copy-done.5
  48.0 0.6 dynamic-slice.1
  48.6 4.0 %all-to-all-done = f32[2,8,75]{2,0,1:T(2,128)S(1)} async-done(((f32[2,8,75]{2,0,1:T(2,128)}), f32[2,8,75]{2,0,1:T(2,128)S(1)}, u32[]{:S(2)}, u32[]{:S(2)}) %all-to-all-start) | async-done | bytes 4832 | tf_op jit(solution)/shard_map/all_to_all | solution.py:37
  52.7 0.6 slice_reduce_fusion
  54.6 0.1 squeeze.8
  54.7 0.0 copy-start.3
  55.3 0.0 copy-done.4
  55.3 0.6 multiply_reduce_fusion.1
  55.9 1.2 %fusion.11 = (f32[1]{0:T(128)}, f32[1]{0:T(128)}) fusion(f32[1]{0:T(128)S(6)} %copy.36, f32[1]{0:T(128)} %bitcast.14, f32[1]{0:T(128)} %bitcast.13), kind=kLoop, calls=%fused_computation.23 | loop fusion | flops 4 | bytes 20 | tf_op jit(solution)/shard_map/sub | solution.py:46
  57.1 1.3 %dynamic-update-slice = f32[4]{0:T(128)S(1)} dynamic-update-slice(f32[4]{0:T(128)S(1)} %broadcast.22, f32[1]{0:T(128)} %get-tuple-element.47, u32[]{:T(128)} %bitcast.15) | dynamic-update-slice | bytes 12
  58.4 5.6 %all-reduce = f32[4]{0:T(128)S(1)} all-reduce(f32[4]{0:T(128)S(1)} %dynamic-update-slice), channel_id=1, replica_groups=mesh['blk'=8,'walk'=4] {'walk'}, use_global_device_ids=true, to_apply=%add | all-reduce | flops 4 | bytes 32
  64.1 0.7 fusion.9
  64.8 1.4 %dynamic-update-slice.1 = f32[8]{0:T(128)S(1)} dynamic-update-slice(f32[8]{0:T(128)S(1)} %broadcast.23, f32[1]{0:T(128)} %bitcast.16, u32[]{:T(128)} %bitcast.17) | dynamic-update-slice | bytes 12
  66.2 17.8 %all-reduce.1 = f32[8]{0:T(128)S(1)} all-reduce(f32[8]{0:T(128)S(1)} %dynamic-update-slice.1), channel_id=1, replica_groups=mesh['blk'=8,'walk'=4] {'blk'}, use_global_device_ids=true, to_apply=%add.1 | all-reduce | flops 8 | bytes 64
  84.0 0.7 fusion.10
  87.2 0.0 copy-done.3
  (6 shorter events, 0.0 us)
Async XLA Ops:
  0.6 35.0 %copy-start = (bf16[75,50,200]{2,0,1:T(8,128)(2,1)S(1)}, bf16[75,50,200]{2,0,1:T(8,128)(2,1)}, u32[]{:S(2)}) copy-start(bf16[75,50,200]{2,0,1:T(8,128)(2,1)} %param.8) | copy-start | bytes 4500004
  35.7 10.5 %copy-start.1 = (bf16[1,50,200]{2,1,0:T(8,128)(2,1)S(1)}, bf16[1,50,200]{2,1,0:T(8,128)(2,1)}, u32[]{:S(2)}) copy-start(bf16[1,50,200]{2,1,0:T(8,128)(2,1)} %param.7) | copy-start | bytes 60004
  35.7 10.5 %copy-start.2 = (f32[50,200]{1,0:T(8,128)S(1)}, f32[50,200]{1,0:T(8,128)}, u32[]{:S(2)}) copy-start(f32[50,200]{1,0:T(8,128)} %param.9) | copy-start | bytes 120004
  35.7 11.8 %copy-start.6 = (u32[32]{0:T(128)S(1)}, u32[32]{0:T(128)}, u32[]{:S(2)}) copy-start(u32[32]{0:T(128)} %constant.48) | copy-start | bytes 388
  35.7 12.3 %copy-start.5 = (u32[32]{0:T(128)S(1)}, u32[32]{0:T(128)}, u32[]{:S(2)}) copy-start(u32[32]{0:T(128)} %constant.53) | copy-start | bytes 388
  35.7 19.6 %copy-start.4 = (f32[1,600]{1,0:T(1,128)S(1)}, f32[1,600]{1,0:T(1,128)}, u32[]{:S(2)}) copy-start(f32[1,600]{1,0:T(1,128)} %param.10) | copy-start | bytes 7204
  40.6 12.0 %all-to-all-start = ((f32[2,8,75]{2,0,1:T(2,128)}), f32[2,8,75]{2,0,1:T(2,128)S(1)}, u32[]{:S(2)}, u32[]{:S(2)}) async-start(f32[2,8,75]{2,0,1:T(2,128)} %copy.14), calls=%async_computation | async-start | bytes 16384 | tf_op jit(solution)/shard_map/all_to_all | solution.py:37
  54.7 32.5 %copy-start.3 = (f32[1,600]{1,0:T(1,128)}, f32[1,600]{1,0:T(1,128)S(1)}, u32[]{:S(2)}) copy-start(f32[1,600]{1,0:T(1,128)S(1)} %squeeze.8) | copy-start | bytes 7204
where the time goes:
time: 89.8 us; the launch traced here: 89.4 us
  blocking collectives  56.2 us (63%)
  between operations  8.12 us (9%)
  other arithmetic  6.73 us (7%)
  starting transfers between devices  5.51 us (6%)
  local copies, waits for them, and re-layouts  4.71 us (5%)
  matrix products  4.05 us (5%)
  waiting for transfers between devices  4.03 us (4%)
    all_gather x1, blocking collectives, on_device(): arrived = lax.all_gather(green_half, 'blk', axis=0, tiled=True)  32.8 us
    unnamed x2, blocking collectives  23.4 us
    all_to_all x1, starting transfers between devices, on_device(): lax.all_to_all(partials, 'blk', split_axis=1, concat_axis=2, tiled=True)  5.51 us
    all_to_all x1, waiting for transfers between devices, on_device(): lax.all_to_all(partials, 'blk', split_axis=1, concat_axis=2, tiled=True)  4.03 us
    unnamed x20, local copies, waits for them, and re-layouts  4 us
    dot_general x2, other arithmetic, crossed_of(): return jnp.einsum('wnij,wnji->wn', table, table)  2.36 us
    dot_general x1, matrix products, on_device(): jnp.einsum('nip,wip->wn', chol_half, arrived, preferred_element_type=jnp....  2.19 us
    dot_general x2, matrix products, crossed_of(): jnp.einsum('nip,wjp->wnij', chol_half, walkers, preferred_element_type=jn...  1.86 us
  transfers between devices with their start and end apart: 1, of which 1 were waited for; matrix products, arithmetic and copies ran while one was open for 2% of the time, Pallas kernels for 0%

commit v1 on v0

v1 whole, which is shorter than its diff:
```python
import functools

import jax
import jax.numpy as jnp
from jax import lax
from jax.experimental import pallas as pl
from jax.experimental.pallas import tpu as pltpu
from jax.sharding import PartitionSpec as P

F32 = jnp.float32
BF16 = jnp.bfloat16
LANES = 128
GROUP = 8


def round_up(value, unit):
    return -(-value // unit) * unit


def split_three(values):
    high = values.astype(BF16)
    rest = values - high.astype(F32)
    middle = rest.astype(BF16)
    low = (rest - middle.astype(F32)).astype(BF16)
    return high, middle, low


def pack_kernel(slab, green_ref, noise_ref, packed_ref):
    blocks, rows, orbitals = packed_ref.shape
    occupied = green_ref.shape[1]
    green = green_ref[0].astype(F32)
    noise = noise_ref[...]
    pad = jnp.zeros((rows - occupied, orbitals), F32)
    base = jnp.concatenate([green, pad], axis=0)
    row = lax.broadcasted_iota(jnp.int32, (rows, orbitals), 0)
    for block in range(blocks):
        piece = noise[:, block * slab : (block + 1) * slab]
        piece = jnp.concatenate([piece, jnp.zeros((1, orbitals - slab), F32)], axis=1)
        value = base
        for k, part in enumerate(split_three(piece)):
            value = jnp.where(row == occupied + k, part.astype(F32), value)
        packed_ref[block] = value.astype(BF16)


def work_kernel(slab, offsets, walk, arrived_ref, green_ref, chol_ref, body_ref, old_ref, send_ref, rows_ref, lhs_ref, rhs_ref, table_ref):
    blocks, rows, orbitals = arrived_ref.shape
    occupied = chol_ref.shape[0]
    pairs = occupied // 2
    folds = send_ref.shape[0] // (blocks * walk)
    wide = folds * LANES
    at_energy, at_exponent, at_old, at_kinetic = offsets
    chunks = [(low, min(low + LANES, orbitals)) for low in range(0, orbitals, LANES)]
    for i in range(occupied):
        rhs_ref[i // 2, (i % 2) * LANES : (i % 2) * LANES + slab, :] = chol_ref[i]
    force, cross, noise = [], [], []
    lane = lax.broadcasted_iota(jnp.int32, (GROUP, LANES), 1)
    for first in range(0, blocks, GROUP):
        for w in range(GROUP):
            for c, (low, high) in enumerate(chunks):
                rows_ref[c, w * rows : (w + 1) * rows, : high - low] = arrived_ref[first + w, :, low:high].astype(F32)
        for j in range(0, occupied, 2):
            for c, (low, high) in enumerate(chunks):
                pair = [rows_ref[c, pl.ds(j + k, GROUP, stride=rows), :] for k in range(2)]
                pair = jnp.concatenate(pair, axis=0).astype(BF16)
                lhs_ref[j * GROUP : (j + 2) * GROUP, low:high] = pair[:, : high - low]
        parts = [rows_ref[0, pl.ds(occupied + k, GROUP, stride=rows), :] for k in range(3)]
        noise.append((parts[0] + parts[1]) + parts[2])
        lhs = lhs_ref[...]

        def fill(p, trace):
            product = lax.dot_general(lhs, rhs_ref[p], (((1,), (1,)), ((), ())), preferred_element_type=F32)
            table_ref[p] = product
            here = pl.multiple_of(p * 2 * GROUP, 2 * GROUP)
            both = table_ref[p, pl.ds(here, 2 * GROUP), :]
            return trace + both[:GROUP, :LANES] + both[GROUP:, LANES:]

        trace = lax.fori_loop(0, pairs, fill, jnp.zeros((GROUP, LANES), F32))

        def exchange(p, total):
            here = pl.multiple_of(p * 2 * GROUP, 2 * GROUP)
            for q in range(pairs):
                mine = table_ref[p, q * 2 * GROUP : (q + 1) * 2 * GROUP, :]
                other = table_ref[q, pl.ds(here, 2 * GROUP), :]
                total = total + mine[:GROUP, :LANES] * other[:GROUP, :LANES]
                total = total + mine[:GROUP, LANES:] * other[GROUP:, :LANES]
                total = total + mine[GROUP:, :LANES] * other[:GROUP, LANES:]
                total = total + mine[GROUP:, LANES:] * other[GROUP:, LANES:]
            return total

        total = lax.fori_loop(0, pairs, exchange, jnp.zeros((GROUP, LANES), F32))
        force.append(jnp.where(lane < slab, trace, 0.0))
        cross.append(jnp.where(lane < slab, total, 0.0))
    force = jnp.concatenate(force, axis=0)
    cross = jnp.concatenate(cross, axis=0)
    noise = jnp.concatenate(noise, axis=0)
    in_slab = lax.broadcasted_iota(jnp.int32, (blocks, LANES), 1) < slab
    shifted = F32(-0.1) * force
    gain = jnp.where(in_slab, noise * shifted + 0.5 * shifted * shifted, 0.0)
    energy = jnp.sum(0.5 * force * force - 0.5 * cross, axis=1, keepdims=True)
    exponent = jnp.sum(gain, axis=1, keepdims=True) - 0.01 * energy
    kinetic = jnp.sum(green_ref[0].astype(F32) * body_ref[...])
    old = old_ref[0]
    if wide > LANES:
        force = jnp.concatenate([force, jnp.zeros((blocks, wide - LANES), F32)], axis=1)
    lane = lax.broadcasted_iota(jnp.int32, (blocks, wide), 1)
    row = lax.broadcasted_iota(jnp.int32, (blocks, wide), 0)
    across = jnp.sum(jnp.where(lane - at_exponent == row, exponent, 0.0), axis=0, keepdims=True)
    message = jnp.where(lane < at_energy, force, energy)
    message = jnp.where(lane >= at_exponent, across, message)
    message = jnp.where(lane >= at_old, old, message)
    message = jnp.where(lane >= at_kinetic, kinetic, message)
    for k in range(walk * folds):
        c = k % folds
        send_ref[pl.ds(k, blocks, stride=walk * folds), :] = message[:, c * LANES : (c + 1) * LANES]


def finish_kernel(slab, offsets, blocks, walk, got_ref, force_ref, energy_ref, weight_ref, comb_ref):
    folds = got_ref.shape[0] // (blocks * walk)
    wide = folds * LANES
    at_energy, at_exponent, at_old, at_kinetic = offsets
    own_block = lax.axis_index("blk")
    own_walk = lax.axis_index("walk")
    lane = lax.broadcasted_iota(jnp.int32, (blocks, wide), 1)
    row = lax.broadcasted_iota(jnp.int32, (blocks, wide), 0)
    keep = (lane < at_old) | (lane - at_old == row) | (lane - at_kinetic == row)
    own = jnp.zeros((blocks, wide), F32)
    sums = []
    for w in range(walk):
        from_w = [got_ref[pl.ds(w * folds + c, blocks, stride=walk * folds), :] for c in range(folds)]
        from_w = jnp.concatenate(from_w, axis=1)
        own = jnp.where(own_walk == w, from_w, own)
        sums.append(jnp.sum(jnp.where(keep, from_w, 0.0), axis=0, keepdims=True))
    for b in range(blocks):
        force_ref[:, b * slab : (b + 1) * slab] = own[b : b + 1, :slab]
    sums = jnp.concatenate(sums, axis=0)
    exponent = sums[:, at_exponent : at_exponent + blocks]
    old = sums[:, at_old : at_old + blocks]
    kinetic = sums[:, at_kinetic : at_kinetic + blocks]
    weight = old * jnp.exp(exponent - 0.01 * kinetic)
    index = lax.broadcasted_iota(jnp.int32, (walk, blocks), 1) * walk + lax.broadcasted_iota(jnp.int32, (walk, blocks), 0)
    rank = own_block * walk + own_walk
    before = jnp.sum(jnp.where(index < rank, weight, 0.0))
    grand = jnp.sum(weight)
    weight_ref[0] = jnp.sum(jnp.where(index == rank, weight, 0.0))
    energy_ref[0] = jnp.sum(jnp.where(lane == at_energy, own, 0.0)) + jnp.sum(jnp.where(index == rank, kinetic, 0.0))
    comb_ref[0] = before * (blocks * walk) / grand - rank.astype(F32)


def on_device(green_half, chol_half, one_body, field_noise, old_weight):
    slab, occupied, orbitals = chol_half.shape
    blocks = lax.axis_size("blk")
    walk = lax.axis_size("walk")
    vmem = pl.BlockSpec(memory_space=pltpu.VMEM)
    smem = pl.BlockSpec(memory_space=pltpu.SMEM)
    rows = round_up(occupied + 3, 8)
    packed = pl.pallas_call(
        functools.partial(pack_kernel, slab),
        out_shape=jax.ShapeDtypeStruct((blocks, rows, orbitals), BF16),
        in_specs=[vmem, vmem],
        out_specs=vmem,
        name="pack",
    )(green_half, field_noise)
    arrived = lax.all_to_all(packed, "blk", split_axis=0, concat_axis=0, tiled=True)
    offsets = (slab, slab + 1, slab + 1 + blocks, slab + 1 + 2 * blocks)
    folds = round_up(slab + 1 + 3 * blocks, LANES) // LANES
    send = pl.pallas_call(
        functools.partial(work_kernel, slab, offsets, walk),
        out_shape=jax.ShapeDtypeStruct((blocks * walk * folds, LANES), F32),
        in_specs=[vmem, vmem, vmem, vmem, smem],
        out_specs=vmem,
        scratch_shapes=[
            pltpu.VMEM((round_up(orbitals, LANES) // LANES, GROUP * rows, LANES), F32),
            pltpu.VMEM((GROUP * occupied, orbitals), BF16),
            pltpu.VMEM((occupied // 2, 2 * LANES, orbitals), BF16),
            pltpu.VMEM((occupied // 2, GROUP * occupied, 2 * LANES), F32),
        ],
        compiler_params=pltpu.CompilerParams(vmem_limit_bytes=40 * 2**20),
        name="work",
    )(arrived, green_half, jnp.swapaxes(chol_half, 0, 1), one_body, old_weight)
    got = lax.all_to_all(send, ("blk", "walk"), split_axis=0, concat_axis=0, tiled=True)
    scalar = jax.ShapeDtypeStruct((1,), F32)
    return tuple(
        pl.pallas_call(
            functools.partial(finish_kernel, slab, offsets, blocks, walk),
            out_shape=(jax.ShapeDtypeStruct((1, slab * blocks), F32), scalar, scalar, scalar),
            in_specs=[vmem],
            out_specs=(vmem, smem, smem, smem),
            name="finish",
        )(got)
    )


def solution(mesh):
    placed = (
        P(("blk", "walk"), None, None),
        P("blk", None, None),
        P(),
        P(("blk", "walk"), None),
        P(("blk", "walk")),
    )
    return jax.shard_map(
        on_device,
        mesh=mesh,
        in_specs=placed,
        out_specs=(
            P(("blk", "walk"), None),
            P(("blk", "walk")),
            P(("blk", "walk")),
            P(("blk", "walk")),
        ),
        check_vma=False,
    )
```

time: 89.8 us -> 43 us (0.48)
  blocking collectives: 56.2 us -> 10.5 us
  Pallas kernels: 0 us -> 12.6 us
  between operations: 8.12 us -> 1.29 us
  other arithmetic: 6.73 us -> 0 us
  matrix products: 4.05 us -> 0 us
  waiting for transfers between devices: 4.03 us -> 7.78 us
  starting transfers between devices: 5.51 us -> 7.25 us
  local copies, waits for them, and re-layouts: 4.71 us -> 3.14 us
    all_gather x1 -> x0, blocking collectives: 32.8 us -> none  [on_device(): arrived = lax.all_gather(green_half, 'blk', axis=0, tiled=True)]
    unnamed x2 -> x0, blocking collectives: 23.4 us -> none
    pallas_call x0 -> x3, Pallas kernels: none -> 12.6 us  [the longest x1 9.43 us: on_device(): pl.pallas_call(functools.partial(work_kernel, slab, offsets, walk), out_s...]
    all_to_all x0 -> x1, blocking collectives: none -> 10.5 us  [on_device(): lax.all_to_all(send, ('blk', 'walk'), split_axis=0, concat_axis=0, tiled=...]
    dot_general x3 -> x0, matrix products: 4.05 us -> none  [the longest x1 2.19 us: on_device(): jnp.einsum('nip,wip->wn', chol_half, arrived, preferred_element_type=jnp....]
    all_to_all x1, waiting for transfers between devices: 4.03 us -> 7.78 us  [on_device(): lax.all_to_all(packed, 'blk', split_axis=0, concat_axis=0, tiled=True)]
    reduce_sum x5 -> x0, other arithmetic: 3.2 us -> none  [the longest x1 0.69 us: lower_sum(): return jnp.sum(jnp.where(ranks < rank_here, values, jnp.float32(0.0)))]
    dot_general x2 -> x0, other arithmetic: 2.36 us -> none  [crossed_of(): return jnp.einsum('wnij,wnji->wn', table, table)]
  transfers between devices with their start and end apart: 1 -> 1, of which waited for: 1 -> 1; matrix products, arithmetic and copies ran while one was open for 2% -> 0% of each run, Pallas kernels for 0% -> 0%
where the time goes in v1:
time: 43 us; the launch traced here: 42.5 us
  Pallas kernels  12.6 us (29%)
  blocking collectives  10.5 us (24%)
  waiting for transfers between devices  7.78 us (18%)
  starting transfers between devices  7.25 us (17%)
  local copies, waits for them, and re-layouts  3.14 us (7%)
  between operations  1.29 us (3%)
    all_to_all x1, blocking collectives, on_device(): lax.all_to_all(send, ('blk', 'walk'), split_axis=0, concat_axis=0, tiled=...  10.5 us
    pallas_call x1, Pallas kernels, on_device(): pl.pallas_call(functools.partial(work_kernel, slab, offsets, walk), out_s...  9.43 us
    all_to_all x1, waiting for transfers between devices, on_device(): lax.all_to_all(packed, 'blk', split_axis=0, concat_axis=0, tiled=True)  7.78 us
    all_to_all x1, starting transfers between devices, on_device(): lax.all_to_all(packed, 'blk', split_axis=0, concat_axis=0, tiled=True)  7.25 us
    unnamed x6, local copies, waits for them, and re-layouts  3.14 us
    pallas_call x1, Pallas kernels, on_device(): pl.pallas_call(functools.partial(finish_kernel, slab, offsets, blocks, wa...  1.62 us
    pallas_call x1, Pallas kernels, on_device(): pl.pallas_call(functools.partial(pack_kernel, slab), out_shape=jax.ShapeD...  1.52 us
  transfers between devices with their start and end apart: 1, of which 1 were waited for; matrix products, arithmetic and copies ran while one was open for 0% of the time, Pallas kernels for 0%

profile of v1, /device:TPU:0, one launch (start us, length us, event | category | flops | bytes accessed | tf_op | source)
XLA Modules:
  0.0 42.5 jit_solution(13485947177776556031)
XLA Ops:
  0.6 1.5 %pack.1 = bf16[8,56,200]{2,1,0:T(8,128)(2,1)} custom-call(bf16[1,50,200]{2,1,0:T(8,128)(2,1)} %green_ref.3, f32[1,600]{1,0:T(1,128)} %noise_ref.1), custom_call_target="tpu_custom_call" | custom-call | tf_op jit(solution)/shard_map/pack/pallas_call | solution.py:156
  2.2 7.3 %all-to-all-start = ((bf16[8,56,200]{2,1,0:T(8,128)(2,1)}), bf16[8,56,200]{2,1,0:T(8,128)(2,1)S(1)}, u32[]{:S(2)}, u32[]{:S(2)}) async-start(bf16[8,56,200]{2,1,0:T(8,128)(2,1)} %pack.1), calls=%async_computation | async-start | bytes 458752 | tf_op jit(solution)/shard_map/all_to_all | solution.py:163
  10.1 7.8 %all-to-all-done.arrived_ref = bf16[8,56,200]{2,1,0:T(8,128)(2,1)S(1)} async-done(((bf16[8,56,200]{2,1,0:T(8,128)(2,1)}), bf16[8,56,200]{2,1,0:T(8,128)(2,1)S(1)}, u32[]{:S(2)}, u32[]{:S(2)}) %all-to-all-start) | async-done | bytes 179232 | tf_op jit(solution)/shard_map/all_to_all | solution.py:163
  17.8 0.0 copy-start
  17.8 1.6 %copy-done = bf16[75,50,200]{2,0,1:T(8,128)(2,1)S(1)} copy-done((bf16[75,50,200]{2,0,1:T(8,128)(2,1)S(1)}, bf16[75,50,200]{2,0,1:T(8,128)(2,1)}, u32[]{:S(2)}) %copy-start) | copy-done | bytes 1500024
  19.4 0.0 copy-start.1
  19.4 0.7 %copy-done.1 = bf16[1,50,200]{2,1,0:T(8,128)(2,1)S(1)} copy-done((bf16[1,50,200]{2,1,0:T(8,128)(2,1)S(1)}, bf16[1,50,200]{2,1,0:T(8,128)(2,1)}, u32[]{:S(2)}) %copy-start.1) | copy-done | bytes 20024
  20.2 0.0 copy-start.2
  20.2 0.8 %copy-done.2 = f32[50,200]{1,0:T(8,128)S(1)} copy-done((f32[50,200]{1,0:T(8,128)S(1)}, f32[50,200]{1,0:T(8,128)}, u32[]{:S(2)}) %copy-start.2) | copy-done | bytes 40024
  21.0 9.4 %work.1 = f32[32,128]{1,0:T(8,128)S(1)} custom-call(bf16[8,56,200]{2,1,0:T(8,128)(2,1)S(1)} %all-to-all-done.arrived_ref, bf16[1,50,200]{2,1,0:T(8,128)(2,1)S(1)} %copy-done.1, bf16[50,75,200]{2,1,0:T(8,128)(2,1)S(1)} %bitcast.5, f32[50,200]{1,0:T(8,128)S(1)} %copy-done.2, f32[1]{0:T(128)S(6)} %copy.10.old_ref), custom_call_target="tpu_custom_call" | custom-call | tf_op jit(solution)/shard_map/work/pallas_call | solution.py:166
  30.4 10.5 %all_to_all.16 = f32[32,1,128]{2,1,0:T(1,128)} all-to-all(f32[32,1,128]{2,1,0:T(1,128)S(1)} %bitcast.6), channel_id=1, replica_groups=mesh['blk'=8,'walk'=4] {'blk','walk'}, dimensions={0} | all-to-all | bytes 32768 | tf_op jit(solution)/shard_map/all_to_all | solution.py:180
  40.9 1.6 %finish.1 = (f32[1,600]{1,0:T(1,128)}, f32[1]{0:T(128)}, f32[1]{0:T(128)}, f32[1]{0:T(128)}) custom-call(f32[32,128]{1,0:T(8,128)} %bitcast.7), custom_call_target="tpu_custom_call" | custom-call | tf_op jit(solution)/shard_map/finish/pallas_call | solution.py:183
Async XLA Ops:
  2.2 15.7 %all-to-all-start = ((bf16[8,56,200]{2,1,0:T(8,128)(2,1)}), bf16[8,56,200]{2,1,0:T(8,128)(2,1)S(1)}, u32[]{:S(2)}, u32[]{:S(2)}) async-start(bf16[8,56,200]{2,1,0:T(8,128)(2,1)} %pack.1), calls=%async_computation | async-start | bytes 458752 | tf_op jit(solution)/shard_map/all_to_all | solution.py:163
  17.8 1.6 %copy-start = (bf16[75,50,200]{2,0,1:T(8,128)(2,1)S(1)}, bf16[75,50,200]{2,0,1:T(8,128)(2,1)}, u32[]{:S(2)}) copy-start(bf16[75,50,200]{2,0,1:T(8,128)(2,1)} %param.6) | copy-start | bytes 4500004
  19.4 0.7 %copy-start.1 = (bf16[1,50,200]{2,1,0:T(8,128)(2,1)S(1)}, bf16[1,50,200]{2,1,0:T(8,128)(2,1)}, u32[]{:S(2)}) copy-start(bf16[1,50,200]{2,1,0:T(8,128)(2,1)} %green_ref.3) | copy-start | bytes 60004
  20.2 0.8 %copy-start.2 = (f32[50,200]{1,0:T(8,128)S(1)}, f32[50,200]{1,0:T(8,128)}, u32[]{:S(2)}) copy-start(f32[50,200]{1,0:T(8,128)} %body_ref.1) | copy-start | bytes 120004

commit v2 on v1

--- a/solution.py
+++ b/solution.py
@@ -42,16 +42,40 @@
         packed_ref[block] = value.astype(BF16)
 
 
-def work_kernel(slab, offsets, walk, arrived_ref, green_ref, chol_ref, body_ref, old_ref, send_ref, rows_ref, lhs_ref, rhs_ref, table_ref):
+def prepare_kernel(slab, green_ref, chol_ref, body_ref, rhs_ref, kinetic_ref):
+    for i in range(chol_ref.shape[0]):
+        rhs_ref[i // 2, (i % 2) * LANES : (i % 2) * LANES + slab, :] = chol_ref[i]
+    kinetic_ref[0] = jnp.sum(green_ref[0].astype(F32) * body_ref[...])
+
+
+def tables_of(lhs, rhs_ref, table_ref):
+    trace = [jnp.zeros((GROUP, LANES), F32) for _ in range(2)]
+    twice = [jnp.zeros((GROUP, LANES), F32) for _ in range(4)]
+    once = jnp.zeros((GROUP, LANES), F32)
+    for p in range(rhs_ref.shape[0]):
+        table_ref[p] = lax.dot_general(lhs, rhs_ref[p], (((1,), (1,)), ((), ())), preferred_element_type=F32)
+        for q in range(p):
+            mine = table_ref[p, q * 2 * GROUP : (q + 1) * 2 * GROUP, :]
+            other = table_ref[q, p * 2 * GROUP : (p + 1) * 2 * GROUP, :]
+            twice[0] += mine[:GROUP, :LANES] * other[:GROUP, :LANES]
+            twice[1] += mine[:GROUP, LANES:] * other[GROUP:, :LANES]
+            twice[2] += mine[GROUP:, :LANES] * other[:GROUP, LANES:]
+            twice[3] += mine[GROUP:, LANES:] * other[GROUP:, LANES:]
+        both = table_ref[p, p * 2 * GROUP : (p + 1) * 2 * GROUP, :]
+        trace[0] += both[:GROUP, :LANES]
+        trace[1] += both[GROUP:, LANES:]
+        once += both[:GROUP, :LANES] * both[:GROUP, :LANES] + both[GROUP:, LANES:] * both[GROUP:, LANES:]
+        twice[0] += both[:GROUP, LANES:] * both[GROUP:, :LANES]
+    return trace[0] + trace[1], once + 2.0 * ((twice[0] + twice[1]) + (twice[2] + twice[3]))
+
+
+def work_kernel(slab, offsets, walk, arrived_ref, rhs_ref, kinetic_ref, old_ref, send_ref, rows_ref, lhs_ref, table_ref):
     blocks, rows, orbitals = arrived_ref.shape
-    occupied = chol_ref.shape[0]
-    pairs = occupied // 2
+    occupied = lhs_ref.shape[0] // GROUP
     folds = send_ref.shape[0] // (blocks * walk)
     wide = folds * LANES
     at_energy, at_exponent, at_old, at_kinetic = offsets
     chunks = [(low, min(low + LANES, orbitals)) for low in range(0, orbitals, LANES)]
-    for i in range(occupied):
-        rhs_ref[i // 2, (i % 2) * LANES : (i % 2) * LANES + slab, :] = chol_ref[i]
     force, cross, noise = [], [], []
     lane = lax.broadcasted_iota(jnp.int32, (GROUP, LANES), 1)
     for first in range(0, blocks, GROUP):
@@ -65,29 +89,7 @@
                 lhs_ref[j * GROUP : (j + 2) * GROUP, low:high] = pair[:, : high - low]
         parts = [rows_ref[0, pl.ds(occupied + k, GROUP, stride=rows), :] for k in range(3)]
         noise.append((parts[0] + parts[1]) + parts[2])
-        lhs = lhs_ref[...]
-
-        def fill(p, trace):
-            product = lax.dot_general(lhs, rhs_ref[p], (((1,), (1,)), ((), ())), preferred_element_type=F32)
-            table_ref[p] = product
-            here = pl.multiple_of(p * 2 * GROUP, 2 * GROUP)
-            both = table_ref[p, pl.ds(here, 2 * GROUP), :]
-            return trace + both[:GROUP, :LANES] + both[GROUP:, LANES:]
-
-        trace = lax.fori_loop(0, pairs, fill, jnp.zeros((GROUP, LANES), F32))
-
-        def exchange(p, total):
-            here = pl.multiple_of(p * 2 * GROUP, 2 * GROUP)
-            for q in range(pairs):
-                mine = table_ref[p, q * 2 * GROUP : (q + 1) * 2 * GROUP, :]
-                other = table_ref[q, pl.ds(here, 2 * GROUP), :]
-                total = total + mine[:GROUP, :LANES] * other[:GROUP, :LANES]
-                total = total + mine[:GROUP, LANES:] * other[GROUP:, :LANES]
-                total = total + mine[GROUP:, :LANES] * other[:GROUP, LANES:]
-                total = total + mine[GROUP:, LANES:] * other[GROUP:, LANES:]
-            return total
-
-        total = lax.fori_loop(0, pairs, exchange, jnp.zeros((GROUP, LANES), F32))
+        trace, total = tables_of(lhs_ref[...], rhs_ref, table_ref)
         force.append(jnp.where(lane < slab, trace, 0.0))
         cross.append(jnp.where(lane < slab, total, 0.0))
     force = jnp.concatenate(force, axis=0)
@@ -98,8 +100,6 @@
     gain = jnp.where(in_slab, noise * shifted + 0.5 * shifted * shifted, 0.0)
     energy = jnp.sum(0.5 * force * force - 0.5 * cross, axis=1, keepdims=True)
     exponent = jnp.sum(gain, axis=1, keepdims=True) - 0.01 * energy
-    kinetic = jnp.sum(green_ref[0].astype(F32) * body_ref[...])
-    old = old_ref[0]
     if wide > LANES:
         force = jnp.concatenate([force, jnp.zeros((blocks, wide - LANES), F32)], axis=1)
     lane = lax.broadcasted_iota(jnp.int32, (blocks, wide), 1)
@@ -107,8 +107,8 @@
     across = jnp.sum(jnp.where(lane - at_exponent == row, exponent, 0.0), axis=0, keepdims=True)
     message = jnp.where(lane < at_energy, force, energy)
     message = jnp.where(lane >= at_exponent, across, message)
-    message = jnp.where(lane >= at_old, old, message)
-    message = jnp.where(lane >= at_kinetic, kinetic, message)
+    message = jnp.where(lane >= at_old, old_ref[0], message)
+    message = jnp.where(lane >= at_kinetic, kinetic_ref[0], message)
     for k in range(walk * folds):
         c = k % folds
         send_ref[pl.ds(k, blocks, stride=walk * folds), :] = message[:, c * LANES : (c + 1) * LANES]
@@ -153,30 +153,43 @@
     vmem = pl.BlockSpec(memory_space=pltpu.VMEM)
     smem = pl.BlockSpec(memory_space=pltpu.SMEM)
     rows = round_up(occupied + 3, 8)
+    pairs = occupied // 2
+    small = pltpu.CompilerParams(vmem_limit_bytes=4 * 2**20)
     packed = pl.pallas_call(
         functools.partial(pack_kernel, slab),
         out_shape=jax.ShapeDtypeStruct((blocks, rows, orbitals), BF16),
         in_specs=[vmem, vmem],
         out_specs=vmem,
+        compiler_params=small,
         name="pack",
     )(green_half, field_noise)
     arrived = lax.all_to_all(packed, "blk", split_axis=0, concat_axis=0, tiled=True)
+    rhs, kinetic = pl.pallas_call(
+        functools.partial(prepare_kernel, slab),
+        out_shape=(
+            jax.ShapeDtypeStruct((pairs, 2 * LANES, orbitals), BF16),
+            jax.ShapeDtypeStruct((1,), F32),
+        ),
+        in_specs=[vmem, vmem, vmem],
+        out_specs=(vmem, smem),
+        compiler_params=pltpu.CompilerParams(vmem_limit_bytes=12 * 2**20),
+        name="prepare",
+    )(green_half, jnp.swapaxes(chol_half, 0, 1), one_body)
     offsets = (slab, slab + 1, slab + 1 + blocks, slab + 1 + 2 * blocks)
     folds = round_up(slab + 1 + 3 * blocks, LANES) // LANES
     send = pl.pallas_call(
         functools.partial(work_kernel, slab, offsets, walk),
         out_shape=jax.ShapeDtypeStruct((blocks * walk * folds, LANES), F32),
-        in_specs=[vmem, vmem, vmem, vmem, smem],
+        in_specs=[vmem, vmem, smem, smem],
         out_specs=vmem,
         scratch_shapes=[
             pltpu.VMEM((round_up(orbitals, LANES) // LANES, GROUP * rows, LANES), F32),
             pltpu.VMEM((GROUP * occupied, orbitals), BF16),
-            pltpu.VMEM((occupied // 2, 2 * LANES, orbitals), BF16),
-            pltpu.VMEM((occupied // 2, GROUP * occupied, 2 * LANES), F32),
+            pltpu.VMEM((pairs, GROUP * occupied, 2 * LANES), F32),
         ],
-        compiler_params=pltpu.CompilerParams(vmem_limit_bytes=40 * 2**20),
+        compiler_params=pltpu.CompilerParams(vmem_limit_bytes=32 * 2**20),
         name="work",
-    )(arrived, green_half, jnp.swapaxes(chol_half, 0, 1), one_body, old_weight)
+    )(arrived, rhs, kinetic, old_weight)
     got = lax.all_to_all(send, ("blk", "walk"), split_axis=0, concat_axis=0, tiled=True)
     scalar = jax.ShapeDtypeStruct((1,), F32)
     return tuple(
@@ -185,6 +198,7 @@
             out_shape=(jax.ShapeDtypeStruct((1, slab * blocks), F32), scalar, scalar, scalar),
             in_specs=[vmem],
             out_specs=(vmem, smem, smem, smem),
+            compiler_params=small,
             name="finish",
         )(got)
     )

time: 43 us -> 32.6 us (0.76)
  Pallas kernels: 12.6 us -> 4.78 us
  waiting for transfers between devices: 7.78 us -> 3.84 us
  local copies, waits for them, and re-layouts: 3.14 us -> 4.56 us
    pallas_call x1, Pallas kernels: 9.43 us -> 2.3 us  [on_device(): pl.pallas_call(functools.partial(work_kernel, slab, offsets, walk), out_s...]
    all_to_all x1, waiting for transfers between devices: 7.78 us -> 3.84 us  [on_device(): lax.all_to_all(packed, 'blk', split_axis=0, concat_axis=0, tiled=True)]
    unnamed x6 -> x10, local copies, waits for them, and re-layouts: 3.14 us -> 4.56 us
    pallas_call x0 -> x1, Pallas kernels: none -> 0.79 us  [on_device(): pl.pallas_call(functools.partial(prepare_kernel, slab), out_shape=(jax.Sh...]
    pallas_call x1, Pallas kernels: 1.52 us -> 0.78 us  [on_device(): pl.pallas_call(functools.partial(pack_kernel, slab), out_shape=jax.ShapeD...]
    pallas_call x1, Pallas kernels: 1.62 us -> 0.9 us  [on_device(): pl.pallas_call(functools.partial(finish_kernel, slab, offsets, blocks, wa...]
  transfers between devices with their start and end apart: 1 -> 1, of which waited for: 1 -> 1; matrix products, arithmetic and copies ran while one was open for 0% -> 0% of each run, Pallas kernels for 0% -> 2%
where the time goes in v2:
time: 32.6 us; the launch traced here: 32.1 us
  blocking collectives  10.4 us (32%)
  starting transfers between devices  7.25 us (22%)
  Pallas kernels  4.78 us (15%)
  local copies, waits for them, and re-layouts  4.56 us (14%)
  waiting for transfers between devices  3.84 us (12%)
  between operations  1.31 us (4%)
    all_to_all x1, blocking collectives, on_device(): lax.all_to_all(send, ('blk', 'walk'), split_axis=0, concat_axis=0, tiled=...  10.4 us
    all_to_all x1, starting transfers between devices, on_device(): lax.all_to_all(packed, 'blk', split_axis=0, concat_axis=0, tiled=True)  7.25 us
    unnamed x10, local copies, waits for them, and re-layouts  4.56 us
    all_to_all x1, waiting for transfers between devices, on_device(): lax.all_to_all(packed, 'blk', split_axis=0, concat_axis=0, tiled=True)  3.84 us
    pallas_call x1, Pallas kernels, on_device(): pl.pallas_call(functools.partial(work_kernel, slab, offsets, walk), out_s...  2.3 us
    pallas_call x1, Pallas kernels, on_device(): pl.pallas_call(functools.partial(finish_kernel, slab, offsets, blocks, wa...  0.9 us
    pallas_call x1, Pallas kernels, on_device(): pl.pallas_call(functools.partial(prepare_kernel, slab), out_shape=(jax.Sh...  0.79 us
    pallas_call x1, Pallas kernels, on_device(): pl.pallas_call(functools.partial(pack_kernel, slab), out_shape=jax.ShapeD...  0.78 us
  transfers between devices with their start and end apart: 1, of which 1 were waited for; matrix products, arithmetic and copies ran while one was open for 0% of the time, Pallas kernels for 2%

profile of v2, /device:TPU:0, one launch (start us, length us, event | category | flops | bytes accessed | tf_op | source)
XLA Modules:
  0.0 32.1 jit_solution(10182396378773278003)
XLA Ops:
  0.6 0.0 copy-start.1
  0.6 0.7 %copy-done.1 = bf16[1,50,200]{2,1,0:T(8,128)(2,1)S(1)} copy-done((bf16[1,50,200]{2,1,0:T(8,128)(2,1)S(1)}, bf16[1,50,200]{2,1,0:T(8,128)(2,1)}, u32[]{:S(2)}) %copy-start.1) | copy-done | bytes 20024
  1.4 0.0 copy-start.4
  1.4 0.7 %copy-done.4 = f32[1,600]{1,0:T(1,128)S(1)} copy-done((f32[1,600]{1,0:T(1,128)S(1)}, f32[1,600]{1,0:T(1,128)}, u32[]{:S(2)}) %copy-start.4) | copy-done | bytes 2424
  2.1 0.8 %pack.1 = bf16[8,56,200]{2,1,0:T(8,128)(2,1)} custom-call(bf16[1,50,200]{2,1,0:T(8,128)(2,1)S(1)} %copy-done.1, f32[1,600]{1,0:T(1,128)S(1)} %copy-done.4), custom_call_target="tpu_custom_call" | custom-call | tf_op jit(solution)/shard_map/pack/pallas_call | solution.py:158
  2.8 7.3 %all-to-all-start = ((bf16[8,56,200]{2,1,0:T(8,128)(2,1)}), bf16[8,56,200]{2,1,0:T(8,128)(2,1)S(1)}, u32[]{:S(2)}, u32[]{:S(2)}) async-start(bf16[8,56,200]{2,1,0:T(8,128)(2,1)} %pack.1), calls=%async_computation | async-start | bytes 458752 | tf_op jit(solution)/shard_map/all_to_all | solution.py:166
  10.8 0.0 copy-start
  10.8 1.6 %copy-done = bf16[75,50,200]{2,0,1:T(8,128)(2,1)S(1)} copy-done((bf16[75,50,200]{2,0,1:T(8,128)(2,1)S(1)}, bf16[75,50,200]{2,0,1:T(8,128)(2,1)}, u32[]{:S(2)}) %copy-start) | copy-done | bytes 1500024
  12.3 0.0 copy-start.2
  12.3 0.7 %copy-done.2 = bf16[1,50,200]{2,1,0:T(8,128)(2,1)S(1)} copy-done((bf16[1,50,200]{2,1,0:T(8,128)(2,1)S(1)}, bf16[1,50,200]{2,1,0:T(8,128)(2,1)}, u32[]{:S(2)}) %copy-start.2) | copy-done | bytes 20024
  13.1 0.0 copy-start.3
  13.1 0.8 %copy-done.3 = f32[50,200]{1,0:T(8,128)S(1)} copy-done((f32[50,200]{1,0:T(8,128)S(1)}, f32[50,200]{1,0:T(8,128)}, u32[]{:S(2)}) %copy-start.3) | copy-done | bytes 40024
  13.9 0.8 %prepare.1 = (bf16[25,256,200]{2,1,0:T(8,128)(2,1)S(1)}, f32[1]{0:T(128)}) custom-call(bf16[1,50,200]{2,1,0:T(8,128)(2,1)S(1)} %copy-done.2, bf16[50,75,200]{2,1,0:T(8,128)(2,1)S(1)} %bitcast.5, f32[50,200]{1,0:T(8,128)S(1)} %copy-done.3), custom_call_target="tpu_custom_call" | custom-call | tf_op jit(solution)/shard_map/prepare/pallas_call | solution.py:167
  14.7 3.8 %all-to-all-done.arrived_ref = bf16[8,56,200]{2,1,0:T(8,128)(2,1)S(1)} async-done(((bf16[8,56,200]{2,1,0:T(8,128)(2,1)}), bf16[8,56,200]{2,1,0:T(8,128)(2,1)S(1)}, u32[]{:S(2)}, u32[]{:S(2)}) %all-to-all-start) | async-done | bytes 179232 | tf_op jit(solution)/shard_map/all_to_all | solution.py:166
  18.5 2.3 %work.1 = f32[32,128]{1,0:T(8,128)S(1)} custom-call(bf16[8,56,200]{2,1,0:T(8,128)(2,1)S(1)} %all-to-all-done.arrived_ref, bf16[25,256,200]{2,1,0:T(8,128)(2,1)S(1)} %get-tuple-element.6.rhs_ref, f32[1]{0:T(128)} %get-tuple-element.7.kinetic_ref, f32[1]{0:T(128)S(6)} %copy.10.old_ref), custom_call_target="tpu_custom_call" | custom-call | tf_op jit(solution)/shard_map/work/pallas_call | solution.py:180
  20.8 10.4 %all_to_all.16 = f32[32,1,128]{2,1,0:T(1,128)S(1)} all-to-all(f32[32,1,128]{2,1,0:T(1,128)S(1)} %bitcast.7), channel_id=1, replica_groups=mesh['blk'=8,'walk'=4] {'blk','walk'}, dimensions={0} | all-to-all | bytes 32768 | tf_op jit(solution)/shard_map/all_to_all | solution.py:193
  31.2 0.9 %finish.1 = (f32[1,600]{1,0:T(1,128)}, f32[1]{0:T(128)}, f32[1]{0:T(128)}, f32[1]{0:T(128)}) custom-call(f32[32,128]{1,0:T(8,128)S(1)} %bitcast.6), custom_call_target="tpu_custom_call" | custom-call | tf_op jit(solution)/shard_map/finish/pallas_call | solution.py:196
Async XLA Ops:
  0.6 0.8 %copy-start.1 = (bf16[1,50,200]{2,1,0:T(8,128)(2,1)S(1)}, bf16[1,50,200]{2,1,0:T(8,128)(2,1)}, u32[]{:S(2)}) copy-start(bf16[1,50,200]{2,1,0:T(8,128)(2,1)} %green_ref.3) | copy-start | bytes 60004
  1.4 0.7 %copy-start.4 = (f32[1,600]{1,0:T(1,128)S(1)}, f32[1,600]{1,0:T(1,128)}, u32[]{:S(2)}) copy-start(f32[1,600]{1,0:T(1,128)} %noise_ref.1) | copy-start | bytes 7204
  2.8 15.7 %all-to-all-start = ((bf16[8,56,200]{2,1,0:T(8,128)(2,1)}), bf16[8,56,200]{2,1,0:T(8,128)(2,1)S(1)}, u32[]{:S(2)}, u32[]{:S(2)}) async-start(bf16[8,56,200]{2,1,0:T(8,128)(2,1)} %pack.1), calls=%async_computation | async-start | bytes 458752 | tf_op jit(solution)/shard_map/all_to_all | solution.py:166
  10.8 1.6 %copy-start = (bf16[75,50,200]{2,0,1:T(8,128)(2,1)S(1)}, bf16[75,50,200]{2,0,1:T(8,128)(2,1)}, u32[]{:S(2)}) copy-start(bf16[75,50,200]{2,0,1:T(8,128)(2,1)} %param.6) | copy-start | bytes 4500004
  12.3 0.7 %copy-start.2 = (bf16[1,50,200]{2,1,0:T(8,128)(2,1)S(1)}, bf16[1,50,200]{2,1,0:T(8,128)(2,1)}, u32[]{:S(2)}) copy-start(bf16[1,50,200]{2,1,0:T(8,128)(2,1)} %green_ref.3) | copy-start | bytes 60004
  13.1 0.8 %copy-start.3 = (f32[50,200]{1,0:T(8,128)S(1)}, f32[50,200]{1,0:T(8,128)}, u32[]{:S(2)}) copy-start(f32[50,200]{1,0:T(8,128)} %body_ref.1) | copy-start | bytes 120004

commit v3 on v2

--- a/solution.py
+++ b/solution.py
@@ -10,6 +10,8 @@
 F32 = jnp.float32
 BF16 = jnp.bfloat16
 LANES = 128
+TILE = 8
+HALF = LANES // 2
 GROUP = 8
 
 
@@ -25,27 +27,69 @@
     return high, middle, low
 
 
-def pack_kernel(slab, green_ref, noise_ref, packed_ref):
-    blocks, rows, orbitals = packed_ref.shape
-    occupied = green_ref.shape[1]
-    green = green_ref[0].astype(F32)
+def packed_rows(occupied):
+    first = round_up(occupied + 3, TILE)
+    return first, round_up(first + TILE, 2 * TILE) // 2
+
+
+def pack_kernel(slab, green_hbm, noise_hbm, packed_hbm, green_ref, noise_ref, rest_ref, packed_ref, in_sems, out_sems):
+    blocks = packed_ref.shape[0]
+    _, occupied, orbitals = green_ref.shape
+    first, second = packed_rows(occupied)
+    copies = [
+        pltpu.make_async_copy(green_hbm, green_ref, in_sems.at[0]),
+        pltpu.make_async_copy(noise_hbm, noise_ref, in_sems.at[1]),
+    ]
+    for copy in copies:
+        copy.start()
+    rest_ref[...] = jnp.zeros_like(rest_ref)
+    for copy in copies:
+        copy.wait()
+    rest_ref[:occupied, : orbitals - LANES] = green_ref[0, :, LANES:].astype(F32)
+    tiles = [rest_ref[t : t + TILE, :] for t in range(0, first, TILE)]
+    half = second // TILE
+    lane = lax.broadcasted_iota(jnp.int32, (TILE, LANES), 1)
+    row = lax.broadcasted_iota(jnp.int32, (TILE, LANES), 0)
+    folded = [jnp.where(lane < HALF, tiles[t], pltpu.roll(tiles[t + half], HALF, 1)) for t in range(half - 1)]
+    ends = tiles[half - 1]
+    for t in range(len(tiles)):
+        moved = pltpu.roll(tiles[t], t * TILE, 1) if t else tiles[t]
+        ends = jnp.where((lane >= HALF + t * TILE) & (lane < HALF + (t + 1) * TILE), moved, ends)
+    whole = green_ref[0, :, :LANES].astype(F32)
+    cut = occupied // TILE * TILE
+    tail = jnp.concatenate([whole[cut:], jnp.zeros((first - occupied, LANES), F32)], axis=0)
     noise = noise_ref[...]
-    pad = jnp.zeros((rows - occupied, orbitals), F32)
-    base = jnp.concatenate([green, pad], axis=0)
-    row = lax.broadcasted_iota(jnp.int32, (rows, orbitals), 0)
+    sends = []
     for block in range(blocks):
         piece = noise[:, block * slab : (block + 1) * slab]
-        piece = jnp.concatenate([piece, jnp.zeros((1, orbitals - slab), F32)], axis=1)
-        value = base
+        piece = jnp.concatenate([piece, jnp.zeros((1, LANES - slab), F32)], axis=1)
+        last = tail
         for k, part in enumerate(split_three(piece)):
-            value = jnp.where(row == occupied + k, part.astype(F32), value)
-        packed_ref[block] = value.astype(BF16)
-
-
-def prepare_kernel(slab, green_ref, chol_ref, body_ref, rhs_ref, kinetic_ref):
+            last = jnp.where(row == occupied - cut + k, part.astype(F32), last)
+        packed_ref[block] = jnp.concatenate([whole[:cut], last, *folded, ends], axis=0).astype(BF16)
+        sends.append(pltpu.make_async_copy(packed_ref.at[block], packed_hbm.at[block], out_sems.at[block]))
+        sends[-1].start()
+    for send in sends:
+        send.wait()
+
+
+def unpack(packed, rows_ref, at, occupied):
+    first, second = packed_rows(occupied)
+    half = second // TILE
+    rows_ref[0, at : at + first, :] = packed[:first]
+    lane = lax.broadcasted_iota(jnp.int32, (TILE, LANES), 1)
+    ends = packed[first + second - TILE :]
+    for t in range(first // TILE):
+        place = first + (t % half) * TILE
+        tile = packed[place : place + TILE]
+        tile = pltpu.roll(tile, HALF, 1) if t >= half else tile
+        end = pltpu.roll(ends, LANES - t * TILE, 1) if t else ends
+        rows_ref[1, at + t * TILE : at + (t + 1) * TILE, :] = jnp.where(lane < HALF, tile, end)
+
+
+def prepare_kernel(slab, chol_ref, rhs_ref):
     for i in range(chol_ref.shape[0]):
         rhs_ref[i // 2, (i % 2) * LANES : (i % 2) * LANES + slab, :] = chol_ref[i]
-    kinetic_ref[0] = jnp.sum(green_ref[0].astype(F32) * body_ref[...])
 
 
 def tables_of(lhs, rhs_ref, table_ref):
@@ -69,24 +113,32 @@
     return trace[0] + trace[1], once + 2.0 * ((twice[0] + twice[1]) + (twice[2] + twice[3]))
 
 
-def work_kernel(slab, offsets, walk, arrived_ref, rhs_ref, kinetic_ref, old_ref, send_ref, rows_ref, lhs_ref, table_ref):
-    blocks, rows, orbitals = arrived_ref.shape
-    occupied = lhs_ref.shape[0] // GROUP
+def work_kernel(slab, offsets, walk, arrived_ref, rhs_ref, body_ref, old_ref, send_ref, rows_ref, lhs_ref, table_ref):
+    blocks = arrived_ref.shape[0]
+    occupied, orbitals = body_ref.shape
+    rows, _ = packed_rows(occupied)
     folds = send_ref.shape[0] // (blocks * walk)
     wide = folds * LANES
     at_energy, at_exponent, at_old, at_kinetic = offsets
     chunks = [(low, min(low + LANES, orbitals)) for low in range(0, orbitals, LANES)]
+    own = lax.axis_index("blk")
+    kinetic = jnp.zeros((1, 1), F32)
     force, cross, noise = [], [], []
     lane = lax.broadcasted_iota(jnp.int32, (GROUP, LANES), 1)
     for first in range(0, blocks, GROUP):
         for w in range(GROUP):
-            for c, (low, high) in enumerate(chunks):
-                rows_ref[c, w * rows : (w + 1) * rows, : high - low] = arrived_ref[first + w, :, low:high].astype(F32)
+            unpack(arrived_ref[first + w].astype(F32), rows_ref, w * rows, occupied)
         for j in range(0, occupied, 2):
             for c, (low, high) in enumerate(chunks):
                 pair = [rows_ref[c, pl.ds(j + k, GROUP, stride=rows), :] for k in range(2)]
                 pair = jnp.concatenate(pair, axis=0).astype(BF16)
                 lhs_ref[j * GROUP : (j + 2) * GROUP, low:high] = pair[:, : high - low]
+        place = pl.multiple_of(lax.rem(own, GROUP) * rows, TILE)
+        here = jnp.zeros((1, 1), F32)
+        for c, (low, high) in enumerate(chunks):
+            mine = rows_ref[c, pl.ds(place, occupied), :][:, : high - low]
+            here += jnp.sum(mine * body_ref[:, low:high], axis=(0, 1), keepdims=True)
+        kinetic = jnp.where(own // GROUP == first // GROUP, here, kinetic)
         parts = [rows_ref[0, pl.ds(occupied + k, GROUP, stride=rows), :] for k in range(3)]
         noise.append((parts[0] + parts[1]) + parts[2])
         trace, total = tables_of(lhs_ref[...], rhs_ref, table_ref)
@@ -107,8 +159,8 @@
     across = jnp.sum(jnp.where(lane - at_exponent == row, exponent, 0.0), axis=0, keepdims=True)
     message = jnp.where(lane < at_energy, force, energy)
     message = jnp.where(lane >= at_exponent, across, message)
-    message = jnp.where(lane >= at_old, old_ref[0], message)
-    message = jnp.where(lane >= at_kinetic, kinetic_ref[0], message)
+    message = jnp.where(lane >= at_old, old_ref[...], message)
+    message = jnp.where(lane >= at_kinetic, kinetic, message)
     for k in range(walk * folds):
         c = k % folds
         send_ref[pl.ds(k, blocks, stride=walk * folds), :] = message[:, c * LANES : (c + 1) * LANES]
@@ -139,11 +191,14 @@
     weight = old * jnp.exp(exponent - 0.01 * kinetic)
     index = lax.broadcasted_iota(jnp.int32, (walk, blocks), 1) * walk + lax.broadcasted_iota(jnp.int32, (walk, blocks), 0)
     rank = own_block * walk + own_walk
-    before = jnp.sum(jnp.where(index < rank, weight, 0.0))
-    grand = jnp.sum(weight)
-    weight_ref[0] = jnp.sum(jnp.where(index == rank, weight, 0.0))
-    energy_ref[0] = jnp.sum(jnp.where(lane == at_energy, own, 0.0)) + jnp.sum(jnp.where(index == rank, kinetic, 0.0))
-    comb_ref[0] = before * (blocks * walk) / grand - rank.astype(F32)
+
+    def total(values):
+        return jnp.sum(values, axis=(0, 1), keepdims=True)
+
+    before = total(jnp.where(index < rank, weight, 0.0))
+    weight_ref[...] = total(jnp.where(index == rank, weight, 0.0))
+    energy_ref[...] = total(jnp.where(lane == at_energy, own, 0.0)) + total(jnp.where(index == rank, kinetic, 0.0))
+    comb_ref[...] = before * (blocks * walk) / total(weight) - rank.astype(F32)
 
 
 def on_device(green_half, chol_half, one_body, field_noise, old_weight):
@@ -151,57 +206,62 @@
     blocks = lax.axis_size("blk")
     walk = lax.axis_size("walk")
     vmem = pl.BlockSpec(memory_space=pltpu.VMEM)
-    smem = pl.BlockSpec(memory_space=pltpu.SMEM)
-    rows = round_up(occupied + 3, 8)
+    hbm = pl.BlockSpec(memory_space=pltpu.HBM)
+    first, second = packed_rows(occupied)
     pairs = occupied // 2
     small = pltpu.CompilerParams(vmem_limit_bytes=4 * 2**20)
+    message = (blocks, first + second, LANES)
     packed = pl.pallas_call(
         functools.partial(pack_kernel, slab),
-        out_shape=jax.ShapeDtypeStruct((blocks, rows, orbitals), BF16),
-        in_specs=[vmem, vmem],
-        out_specs=vmem,
-        compiler_params=small,
+        out_shape=jax.ShapeDtypeStruct(message, BF16),
+        in_specs=[hbm, hbm],
+        out_specs=hbm,
+        scratch_shapes=[
+            pltpu.VMEM(green_half.shape, BF16),
+            pltpu.VMEM(field_noise.shape, F32),
+            pltpu.VMEM((first, LANES), F32),
+            pltpu.VMEM(message, BF16),
+            pltpu.SemaphoreType.DMA((2,)),
+            pltpu.SemaphoreType.DMA((blocks,)),
+        ],
+        compiler_params=pltpu.CompilerParams(vmem_limit_bytes=60 * 2**20),
         name="pack",
     )(green_half, field_noise)
     arrived = lax.all_to_all(packed, "blk", split_axis=0, concat_axis=0, tiled=True)
-    rhs, kinetic = pl.pallas_call(
+    rhs = pl.pallas_call(
         functools.partial(prepare_kernel, slab),
-        out_shape=(
-            jax.ShapeDtypeStruct((pairs, 2 * LANES, orbitals), BF16),
-            jax.ShapeDtypeStruct((1,), F32),
-        ),
-        in_specs=[vmem, vmem, vmem],
-        out_specs=(vmem, smem),
+        out_shape=jax.ShapeDtypeStruct((pairs, 2 * LANES, orbitals), BF16),
+        in_specs=[vmem],
+        out_specs=vmem,
         compiler_params=pltpu.CompilerParams(vmem_limit_bytes=12 * 2**20),
         name="prepare",
-    )(green_half, jnp.swapaxes(chol_half, 0, 1), one_body)
+    )(jnp.swapaxes(chol_half, 0, 1))
     offsets = (slab, slab + 1, slab + 1 + blocks, slab + 1 + 2 * blocks)
     folds = round_up(slab + 1 + 3 * blocks, LANES) // LANES
     send = pl.pallas_call(
         functools.partial(work_kernel, slab, offsets, walk),
         out_shape=jax.ShapeDtypeStruct((blocks * walk * folds, LANES), F32),
-        in_specs=[vmem, vmem, smem, smem],
+        in_specs=[vmem] * 4,
         out_specs=vmem,
         scratch_shapes=[
-            pltpu.VMEM((round_up(orbitals, LANES) // LANES, GROUP * rows, LANES), F32),
+            pltpu.VMEM((round_up(orbitals, LANES) // LANES, GROUP * first, LANES), F32),
             pltpu.VMEM((GROUP * occupied, orbitals), BF16),
             pltpu.VMEM((pairs, GROUP * occupied, 2 * LANES), F32),
         ],
         compiler_params=pltpu.CompilerParams(vmem_limit_bytes=32 * 2**20),
         name="work",
-    )(arrived, rhs, kinetic, old_weight)
+    )(arrived, rhs, one_body, old_weight.reshape(1, 1))
     got = lax.all_to_all(send, ("blk", "walk"), split_axis=0, concat_axis=0, tiled=True)
-    scalar = jax.ShapeDtypeStruct((1,), F32)
-    return tuple(
-        pl.pallas_call(
-            functools.partial(finish_kernel, slab, offsets, blocks, walk),
-            out_shape=(jax.ShapeDtypeStruct((1, slab * blocks), F32), scalar, scalar, scalar),
-            in_specs=[vmem],
-            out_specs=(vmem, smem, smem, smem),
-            compiler_params=small,
-            name="finish",
-        )(got)
-    )
+    one = jax.ShapeDtypeStruct((1, 1), F32)
+    force, energy, weight, comb = pl.pallas_call(
+        functools.partial(finish_kernel, slab, offsets, blocks, walk),
+        out_shape=(jax.ShapeDtypeStruct((1, slab * blocks), F32), one, one, one),
+        in_specs=[vmem],
+        out_specs=(vmem,) * 4,
+        compiler_params=small,
+        name="finish",
+    )(got)
+    return force, energy.reshape(1), weight.reshape(1), comb.reshape(1)
 
 
 def solution(mesh):

time: 32.6 us -> 30.2 us (0.926)
  local copies, waits for them, and re-layouts: 4.56 us -> 1.57 us
  waiting for transfers between devices: 3.84 us -> 5.32 us
  Pallas kernels: 4.78 us -> 4.36 us
  blocking collectives: 10.4 us -> 10 us
    unnamed x10 -> x4, local copies, waits for them, and re-layouts: 4.56 us -> 1.57 us
    all_to_all x1, waiting for transfers between devices: 3.84 us -> 5.32 us  [on_device(): lax.all_to_all(packed, 'blk', split_axis=0, concat_axis=0, tiled=True)]
    pallas_call x1, Pallas kernels: 0.78 us -> 1.62 us  [on_device(): pl.pallas_call(functools.partial(pack_kernel, slab), out_shape=jax.ShapeD...]
    pallas_call x1, Pallas kernels: 0.79 us -> 0.15 us  [on_device(): pl.pallas_call(functools.partial(prepare_kernel, slab), out_shape=jax.Sha...]
    pallas_call x1, Pallas kernels: 2.3 us -> 1.7 us  [on_device(): pl.pallas_call(functools.partial(work_kernel, slab, offsets, walk), out_s...]
  transfers between devices with their start and end apart: 1 -> 1, of which waited for: 1 -> 1; matrix products, arithmetic and copies ran while one was open for 0% -> 0% of each run, Pallas kernels for 2% -> 1%
where the time goes in v3:
time: 30.2 us; the launch traced here: 29.9 us
  blocking collectives  10 us (33%)
  starting transfers between devices  7.26 us (24%)
  waiting for transfers between devices  5.32 us (18%)
  Pallas kernels  4.36 us (14%)
  local copies, waits for them, and re-layouts  1.57 us (5%)
  between operations  1.31 us (4%)
    all_to_all x1, blocking collectives, on_device(): lax.all_to_all(send, ('blk', 'walk'), split_axis=0, concat_axis=0, tiled=...  10 us
    all_to_all x1, starting transfers between devices, on_device(): lax.all_to_all(packed, 'blk', split_axis=0, concat_axis=0, tiled=True)  7.26 us
    all_to_all x1, waiting for transfers between devices, on_device(): lax.all_to_all(packed, 'blk', split_axis=0, concat_axis=0, tiled=True)  5.32 us
    pallas_call x1, Pallas kernels, on_device(): pl.pallas_call(functools.partial(work_kernel, slab, offsets, walk), out_s...  1.7 us
    pallas_call x1, Pallas kernels, on_device(): pl.pallas_call(functools.partial(pack_kernel, slab), out_shape=jax.ShapeD...  1.62 us
    unnamed x4, local copies, waits for them, and re-layouts  1.57 us
    pallas_call x1, Pallas kernels, on_device(): pl.pallas_call(functools.partial(finish_kernel, slab, offsets, blocks, wa...  0.89 us
  transfers between devices with their start and end apart: 1, of which 1 were waited for; matrix products, arithmetic and copies ran while one was open for 0% of the time, Pallas kernels for 1%

profile of v3, /device:TPU:0, one launch (start us, length us, event | category | flops | bytes accessed | tf_op | source)
XLA Modules:
  0.0 29.9 jit_solution(9590191313080411195)
XLA Ops:
  0.6 0.0 copy-start.1
  0.6 1.6 %pack.1 = bf16[8,88,128]{2,1,0:T(8,128)(2,1)} custom-call(bf16[1,50,200]{2,1,0:T(8,128)(2,1)} %green_hbm.1, f32[1,600]{1,0:T(1,128)} %noise_hbm.1), custom_call_target="tpu_custom_call" | custom-call | tf_op jit(solution)/shard_map/pack/pallas_call | solution.py:214
  2.3 7.3 %all-to-all-start = ((bf16[8,88,128]{2,1,0:T(8,128)(2,1)}), bf16[8,88,128]{2,1,0:T(8,128)(2,1)S(1)}, u32[]{:S(2)}, u32[]{:S(2)}) async-start(bf16[8,88,128]{2,1,0:T(8,128)(2,1)} %pack.1), calls=%async_computation | async-start | bytes 360448 | tf_op jit(solution)/shard_map/all_to_all | solution.py:230
  10.2 0.0 copy-start
  10.2 1.6 %copy-done = bf16[75,50,200]{2,0,1:T(8,128)(2,1)S(1)} copy-done((bf16[75,50,200]{2,0,1:T(8,128)(2,1)S(1)}, bf16[75,50,200]{2,0,1:T(8,128)(2,1)}, u32[]{:S(2)}) %copy-start) | copy-done | bytes 1500024
  11.8 0.2 prepare.1.rhs_ref
  11.9 5.3 %all-to-all-done.arrived_ref = bf16[8,88,128]{2,1,0:T(8,128)(2,1)S(1)} async-done(((bf16[8,88,128]{2,1,0:T(8,128)(2,1)}), bf16[8,88,128]{2,1,0:T(8,128)(2,1)S(1)}, u32[]{:S(2)}, u32[]{:S(2)}) %all-to-all-start) | async-done | bytes 180256 | tf_op jit(solution)/shard_map/all_to_all | solution.py:230
  17.2 0.0 copy-done.1
  17.2 1.7 %work.1 = f32[32,128]{1,0:T(8,128)S(1)} custom-call(bf16[8,88,128]{2,1,0:T(8,128)(2,1)S(1)} %all-to-all-done.arrived_ref, bf16[25,256,200]{2,1,0:T(8,128)(2,1)S(1)} %prepare.1.rhs_ref, f32[50,200]{1,0:T(8,128)S(1)} %copy-done.1, f32[1,1]{1,0:T(1,128)} %bitcast.9.old_ref), custom_call_target="tpu_custom_call" | custom-call | tf_op jit(solution)/shard_map/work/pallas_call | solution.py:241
  18.9 10.0 %all_to_all.16 = f32[32,1,128]{2,1,0:T(1,128)S(1)} all-to-all(f32[32,1,128]{2,1,0:T(1,128)S(1)} %bitcast.12), channel_id=1, replica_groups=mesh['blk'=8,'walk'=4] {'blk','walk'}, dimensions={0} | all-to-all | bytes 32768 | tf_op jit(solution)/shard_map/all_to_all | solution.py:254
  29.0 0.9 %finish.1 = (f32[1,600]{1,0:T(1,128)}, f32[1,1]{1,0:T(1,128)}, f32[1,1]{1,0:T(1,128)}, f32[1,1]{1,0:T(1,128)}) custom-call(f32[32,128]{1,0:T(8,128)S(1)} %bitcast.11), custom_call_target="tpu_custom_call" | custom-call | tf_op jit(solution)/shard_map/finish/pallas_call | solution.py:256
Async XLA Ops:
  0.6 16.6 %copy-start.1 = (f32[50,200]{1,0:T(8,128)S(1)}, f32[50,200]{1,0:T(8,128)}, u32[]{:S(2)}) copy-start(f32[50,200]{1,0:T(8,128)} %body_ref.1) | copy-start | bytes 120004
  2.3 15.0 %all-to-all-start = ((bf16[8,88,128]{2,1,0:T(8,128)(2,1)}), bf16[8,88,128]{2,1,0:T(8,128)(2,1)S(1)}, u32[]{:S(2)}, u32[]{:S(2)}) async-start(bf16[8,88,128]{2,1,0:T(8,128)(2,1)} %pack.1), calls=%async_computation | async-start | bytes 360448 | tf_op jit(solution)/shard_map/all_to_all | solution.py:230
  10.2 1.6 %copy-start = (bf16[75,50,200]{2,0,1:T(8,128)(2,1)S(1)}, bf16[75,50,200]{2,0,1:T(8,128)(2,1)}, u32[]{:S(2)}) copy-start(bf16[75,50,200]{2,0,1:T(8,128)(2,1)} %param.6) | copy-start | bytes 4500004

commit v4 on v3

--- a/solution.py
+++ b/solution.py
@@ -27,13 +27,20 @@
     return high, middle, low
 
 
+def exchange_order(blocks):
+    if blocks % 4:
+        return list(range(blocks))
+    lines = blocks // 2
+    line = [z for pair in zip(range(lines // 2 - 1, -1, -1), range(lines - 1, lines // 2 - 1, -1)) for z in pair]
+    return [2 * z + x for x in (1, 0) for z in line]
+
+
 def packed_rows(occupied):
     first = round_up(occupied + 3, TILE)
     return first, round_up(first + TILE, 2 * TILE) // 2
 
 
-def pack_kernel(slab, green_hbm, noise_hbm, packed_hbm, green_ref, noise_ref, rest_ref, packed_ref, in_sems, out_sems):
-    blocks = packed_ref.shape[0]
+def pack_kernel(slab, order, green_hbm, noise_hbm, packed_hbm, green_ref, noise_ref, rest_ref, packed_ref, in_sems, out_sems):
     _, occupied, orbitals = green_ref.shape
     first, second = packed_rows(occupied)
     copies = [
@@ -60,14 +67,14 @@
     tail = jnp.concatenate([whole[cut:], jnp.zeros((first - occupied, LANES), F32)], axis=0)
     noise = noise_ref[...]
     sends = []
-    for block in range(blocks):
+    for slot, block in enumerate(order):
         piece = noise[:, block * slab : (block + 1) * slab]
         piece = jnp.concatenate([piece, jnp.zeros((1, LANES - slab), F32)], axis=1)
         last = tail
         for k, part in enumerate(split_three(piece)):
             last = jnp.where(row == occupied - cut + k, part.astype(F32), last)
-        packed_ref[block] = jnp.concatenate([whole[:cut], last, *folded, ends], axis=0).astype(BF16)
-        sends.append(pltpu.make_async_copy(packed_ref.at[block], packed_hbm.at[block], out_sems.at[block]))
+        packed_ref[slot] = jnp.concatenate([whole[:cut], last, *folded, ends], axis=0).astype(BF16)
+        sends.append(pltpu.make_async_copy(packed_ref.at[slot], packed_hbm.at[slot], out_sems.at[slot]))
         sends[-1].start()
     for send in sends:
         send.wait()
@@ -113,7 +120,7 @@
     return trace[0] + trace[1], once + 2.0 * ((twice[0] + twice[1]) + (twice[2] + twice[3]))
 
 
-def work_kernel(slab, offsets, walk, arrived_ref, rhs_ref, body_ref, old_ref, send_ref, rows_ref, lhs_ref, table_ref):
+def work_kernel(slab, order, offsets, walk, arrived_ref, rhs_ref, body_ref, old_ref, send_ref, rows_ref, lhs_ref, table_ref):
     blocks = arrived_ref.shape[0]
     occupied, orbitals = body_ref.shape
     rows, _ = packed_rows(occupied)
@@ -127,7 +134,7 @@
     lane = lax.broadcasted_iota(jnp.int32, (GROUP, LANES), 1)
     for first in range(0, blocks, GROUP):
         for w in range(GROUP):
-            unpack(arrived_ref[first + w].astype(F32), rows_ref, w * rows, occupied)
+            unpack(arrived_ref[order.index(first + w)].astype(F32), rows_ref, w * rows, occupied)
         for j in range(0, occupied, 2):
             for c, (low, high) in enumerate(chunks):
                 pair = [rows_ref[c, pl.ds(j + k, GROUP, stride=rows), :] for k in range(2)]
@@ -205,6 +212,7 @@
     slab, occupied, orbitals = chol_half.shape
     blocks = lax.axis_size("blk")
     walk = lax.axis_size("walk")
+    order = exchange_order(blocks)
     vmem = pl.BlockSpec(memory_space=pltpu.VMEM)
     hbm = pl.BlockSpec(memory_space=pltpu.HBM)
     first, second = packed_rows(occupied)
@@ -212,7 +220,7 @@
     small = pltpu.CompilerParams(vmem_limit_bytes=4 * 2**20)
     message = (blocks, first + second, LANES)
     packed = pl.pallas_call(
-        functools.partial(pack_kernel, slab),
+        functools.partial(pack_kernel, slab, order),
         out_shape=jax.ShapeDtypeStruct(message, BF16),
         in_specs=[hbm, hbm],
         out_specs=hbm,
@@ -227,7 +235,7 @@
         compiler_params=pltpu.CompilerParams(vmem_limit_bytes=60 * 2**20),
         name="pack",
     )(green_half, field_noise)
-    arrived = lax.all_to_all(packed, "blk", split_axis=0, concat_axis=0, tiled=True)
+    arrived = lax.all_to_all(packed, "blk", split_axis=0, concat_axis=0, axis_index_groups=[order], tiled=True)
     rhs = pl.pallas_call(
         functools.partial(prepare_kernel, slab),
         out_shape=jax.ShapeDtypeStruct((pairs, 2 * LANES, orbitals), BF16),
@@ -239,7 +247,7 @@
     offsets = (slab, slab + 1, slab + 1 + blocks, slab + 1 + 2 * blocks)
     folds = round_up(slab + 1 + 3 * blocks, LANES) // LANES
     send = pl.pallas_call(
-        functools.partial(work_kernel, slab, offsets, walk),
+        functools.partial(work_kernel, slab, order, offsets, walk),
         out_shape=jax.ShapeDtypeStruct((blocks * walk * folds, LANES), F32),
         in_specs=[vmem] * 4,
         out_specs=vmem,

time: 30.2 us -> 28.6 us (0.947)
  waiting for transfers between devices: 5.32 us -> 3.27 us
  starting transfers between devices: 7.26 us -> 7.83 us
    all_to_all x1, waiting for transfers between devices: 5.32 us -> 3.27 us  [on_device(): lax.all_to_all(packed, 'blk', split_axis=0, concat_axis=0, axis_index_gro...]
    all_to_all x1, starting transfers between devices: 7.26 us -> 7.83 us  [on_device(): lax.all_to_all(packed, 'blk', split_axis=0, concat_axis=0, axis_index_gro...]
where the time goes in v4:
time: 28.6 us; the launch traced here: 28.2 us
  blocking collectives  9.91 us (35%)
  starting transfers between devices  7.83 us (27%)
  Pallas kernels  4.35 us (15%)
  waiting for transfers between devices  3.27 us (11%)
  local copies, waits for them, and re-layouts  1.57 us (5%)
  between operations  1.31 us (5%)
    all_to_all x1, blocking collectives, on_device(): lax.all_to_all(send, ('blk', 'walk'), split_axis=0, concat_axis=0, tiled=...  9.91 us
    all_to_all x1, starting transfers between devices, on_device(): lax.all_to_all(packed, 'blk', split_axis=0, concat_axis=0, axis_index_gro...  7.83 us
    all_to_all x1, waiting for transfers between devices, on_device(): lax.all_to_all(packed, 'blk', split_axis=0, concat_axis=0, axis_index_gro...  3.27 us
    pallas_call x1, Pallas kernels, on_device(): pl.pallas_call(functools.partial(work_kernel, slab, order, offsets, walk)...  1.69 us
    pallas_call x1, Pallas kernels, on_device(): pl.pallas_call(functools.partial(pack_kernel, slab, order), out_shape=jax...  1.62 us
    unnamed x4, local copies, waits for them, and re-layouts  1.57 us
    pallas_call x1, Pallas kernels, on_device(): pl.pallas_call(functools.partial(finish_kernel, slab, offsets, blocks, wa...  0.89 us
  transfers between devices with their start and end apart: 1, of which 1 were waited for; matrix products, arithmetic and copies ran while one was open for 0% of the time, Pallas kernels for 1%

profile of v4, /device:TPU:0, one launch (start us, length us, event | category | flops | bytes accessed | tf_op | source)
XLA Modules:
  0.0 28.2 jit_solution(7049229866856354683)
XLA Ops:
  0.6 0.0 copy-start.1
  0.6 1.6 %pack.1 = bf16[8,88,128]{2,1,0:T(8,128)(2,1)} custom-call(bf16[1,50,200]{2,1,0:T(8,128)(2,1)} %green_hbm.1, f32[1,600]{1,0:T(1,128)} %noise_hbm.1), custom_call_target="tpu_custom_call" | custom-call | tf_op jit(solution)/shard_map/pack/pallas_call | solution.py:222
  2.3 7.8 %all-to-all-start = ((bf16[8,88,128]{2,1,0:T(8,128)(2,1)}), bf16[8,88,128]{2,1,0:T(8,128)(2,1)S(1)}, u32[]{:S(2)}, u32[]{:S(2)}) async-start(bf16[8,88,128]{2,1,0:T(8,128)(2,1)} %pack.1), calls=%async_computation | async-start | bytes 360448 | tf_op jit(solution)/shard_map/all_to_all | solution.py:238
  10.7 0.0 copy-start
  10.8 1.6 %copy-done = bf16[75,50,200]{2,0,1:T(8,128)(2,1)S(1)} copy-done((bf16[75,50,200]{2,0,1:T(8,128)(2,1)S(1)}, bf16[75,50,200]{2,0,1:T(8,128)(2,1)}, u32[]{:S(2)}) %copy-start) | copy-done | bytes 1500024
  12.3 0.2 prepare.1.rhs_ref
  12.5 3.3 %all-to-all-done.arrived_ref = bf16[8,88,128]{2,1,0:T(8,128)(2,1)S(1)} async-done(((bf16[8,88,128]{2,1,0:T(8,128)(2,1)}), bf16[8,88,128]{2,1,0:T(8,128)(2,1)S(1)}, u32[]{:S(2)}, u32[]{:S(2)}) %all-to-all-start) | async-done | bytes 180256 | tf_op jit(solution)/shard_map/all_to_all | solution.py:238
  15.7 0.0 copy-done.1
  15.7 1.7 %work.1 = f32[32,128]{1,0:T(8,128)S(1)} custom-call(bf16[8,88,128]{2,1,0:T(8,128)(2,1)S(1)} %all-to-all-done.arrived_ref, bf16[25,256,200]{2,1,0:T(8,128)(2,1)S(1)} %prepare.1.rhs_ref, f32[50,200]{1,0:T(8,128)S(1)} %copy-done.1, f32[1,1]{1,0:T(1,128)} %bitcast.9.old_ref), custom_call_target="tpu_custom_call" | custom-call | tf_op jit(solution)/shard_map/work/pallas_call | solution.py:249
  17.4 9.9 %all_to_all.16 = f32[32,1,128]{2,1,0:T(1,128)S(1)} all-to-all(f32[32,1,128]{2,1,0:T(1,128)S(1)} %bitcast.12), channel_id=1, replica_groups=mesh['blk'=8,'walk'=4] {'blk','walk'}, dimensions={0} | all-to-all | bytes 32768 | tf_op jit(solution)/shard_map/all_to_all | solution.py:262
  27.4 0.9 %finish.1 = (f32[1,600]{1,0:T(1,128)}, f32[1,1]{1,0:T(1,128)}, f32[1,1]{1,0:T(1,128)}, f32[1,1]{1,0:T(1,128)}) custom-call(f32[32,128]{1,0:T(8,128)S(1)} %bitcast.11), custom_call_target="tpu_custom_call" | custom-call | tf_op jit(solution)/shard_map/finish/pallas_call | solution.py:264
Async XLA Ops:
  0.6 15.1 %copy-start.1 = (f32[50,200]{1,0:T(8,128)S(1)}, f32[50,200]{1,0:T(8,128)}, u32[]{:S(2)}) copy-start(f32[50,200]{1,0:T(8,128)} %body_ref.1) | copy-start | bytes 120004
  2.3 13.5 %all-to-all-start = ((bf16[8,88,128]{2,1,0:T(8,128)(2,1)}), bf16[8,88,128]{2,1,0:T(8,128)(2,1)S(1)}, u32[]{:S(2)}, u32[]{:S(2)}) async-start(bf16[8,88,128]{2,1,0:T(8,128)(2,1)} %pack.1), calls=%async_computation | async-start | bytes 360448 | tf_op jit(solution)/shard_map/all_to_all | solution.py:238
  10.7 1.6 %copy-start = (bf16[75,50,200]{2,0,1:T(8,128)(2,1)S(1)}, bf16[75,50,200]{2,0,1:T(8,128)(2,1)}, u32[]{:S(2)}) copy-start(bf16[75,50,200]{2,0,1:T(8,128)(2,1)} %param.6) | copy-start | bytes 4500004

commit v5 on v4

--- a/solution.py
+++ b/solution.py
@@ -30,68 +30,75 @@
 def exchange_order(blocks):
     if blocks % 4:
         return list(range(blocks))
-    lines = blocks // 2
-    line = [z for pair in zip(range(lines // 2 - 1, -1, -1), range(lines - 1, lines // 2 - 1, -1)) for z in pair]
-    return [2 * z + x for x in (1, 0) for z in line]
-
-
-def packed_rows(occupied):
-    first = round_up(occupied + 3, TILE)
-    return first, round_up(first + TILE, 2 * TILE) // 2
-
-
-def pack_kernel(slab, order, green_hbm, noise_hbm, packed_hbm, green_ref, noise_ref, rest_ref, packed_ref, in_sems, out_sems):
-    _, occupied, orbitals = green_ref.shape
-    first, second = packed_rows(occupied)
+    half = blocks // 4
+    return [2 * z + x for low in range(half - 1, -1, -1) for x in (1, 0) for z in (low, low + half)]
+
+
+MESSAGE = 80
+STRIDE = 56
+SIDE = 48
+
+
+def tile_iotas():
+    shape = (TILE, LANES)
+    return lax.broadcasted_iota(jnp.int32, shape, 0), lax.broadcasted_iota(jnp.int32, shape, 1)
+
+
+def turned(tile, lanes=0, rows=0):
+    tile = pltpu.roll(tile, lanes % LANES, 1) if lanes % LANES else tile
+    return pltpu.roll(tile, rows % TILE, 0) if rows % TILE else tile
+
+
+def pack_kernel(slab, order, green_hbm, noise_hbm, packed_hbm, green_ref, noise_ref, wide_ref, packed_ref, in_sems, out_sems):
+    occupied, orbitals = green_ref.shape[1:]
     copies = [
         pltpu.make_async_copy(green_hbm, green_ref, in_sems.at[0]),
         pltpu.make_async_copy(noise_hbm, noise_ref, in_sems.at[1]),
     ]
     for copy in copies:
         copy.start()
-    rest_ref[...] = jnp.zeros_like(rest_ref)
+    wide_ref[...] = jnp.zeros_like(wide_ref)
     for copy in copies:
         copy.wait()
-    rest_ref[:occupied, : orbitals - LANES] = green_ref[0, :, LANES:].astype(F32)
-    tiles = [rest_ref[t : t + TILE, :] for t in range(0, first, TILE)]
-    half = second // TILE
-    lane = lax.broadcasted_iota(jnp.int32, (TILE, LANES), 1)
-    row = lax.broadcasted_iota(jnp.int32, (TILE, LANES), 0)
-    folded = [jnp.where(lane < HALF, tiles[t], pltpu.roll(tiles[t + half], HALF, 1)) for t in range(half - 1)]
-    ends = tiles[half - 1]
-    for t in range(len(tiles)):
-        moved = pltpu.roll(tiles[t], t * TILE, 1) if t else tiles[t]
-        ends = jnp.where((lane >= HALF + t * TILE) & (lane < HALF + (t + 1) * TILE), moved, ends)
-    whole = green_ref[0, :, :LANES].astype(F32)
-    cut = occupied // TILE * TILE
-    tail = jnp.concatenate([whole[cut:], jnp.zeros((first - occupied, LANES), F32)], axis=0)
+    wide_ref[0, :occupied, :] = green_ref[0, :, :LANES].astype(F32)
+    wide_ref[1, :occupied, : orbitals - LANES] = green_ref[0, :, LANES:].astype(F32)
+    rest = [wide_ref[1, t * TILE : (t + 1) * TILE, :] for t in range(STRIDE // TILE)]
+    row, lane = tile_iotas()
+    folded = [jnp.where(lane < HALF, rest[t], turned(rest[t + 3], HALF)) for t in range(3)]
+    last, after = wide_ref[0, SIDE:STRIDE, :], rest[6]
+    side = turned(last, SIDE)
+    side = jnp.where((row == 2) | (row == 3), jnp.where(lane < 96, turned(last, -32, 2), turned(after, 56, 2)), side)
+    side = jnp.where(row == 4, jnp.where(lane < 88, turned(after, SIDE, 4), turned(after, 88, 3)), side)
+    for t in range(6):
+        side = jnp.where((lane >= t * TILE) & (lane < (t + 1) * TILE), turned(rest[t], t * TILE - HALF), side)
+    whole = wide_ref[0, :SIDE, :]
     noise = noise_ref[...]
     sends = []
     for slot, block in enumerate(order):
         piece = noise[:, block * slab : (block + 1) * slab]
-        piece = jnp.concatenate([piece, jnp.zeros((1, LANES - slab), F32)], axis=1)
-        last = tail
+        piece = jnp.concatenate([jnp.zeros((1, SIDE), F32), piece, jnp.zeros((1, LANES - SIDE - slab), F32)], axis=1)
+        final = side
         for k, part in enumerate(split_three(piece)):
-            last = jnp.where(row == occupied - cut + k, part.astype(F32), last)
-        packed_ref[slot] = jnp.concatenate([whole[:cut], last, *folded, ends], axis=0).astype(BF16)
+            final = jnp.where((row == 5 + k) & (lane >= SIDE), part.astype(F32), final)
+        packed_ref[slot] = jnp.concatenate([whole, *folded, final], axis=0).astype(BF16)
         sends.append(pltpu.make_async_copy(packed_ref.at[slot], packed_hbm.at[slot], out_sems.at[slot]))
         sends[-1].start()
     for send in sends:
         send.wait()
 
 
-def unpack(packed, rows_ref, at, occupied):
-    first, second = packed_rows(occupied)
-    half = second // TILE
-    rows_ref[0, at : at + first, :] = packed[:first]
-    lane = lax.broadcasted_iota(jnp.int32, (TILE, LANES), 1)
-    ends = packed[first + second - TILE :]
-    for t in range(first // TILE):
-        place = first + (t % half) * TILE
-        tile = packed[place : place + TILE]
-        tile = pltpu.roll(tile, HALF, 1) if t >= half else tile
-        end = pltpu.roll(ends, LANES - t * TILE, 1) if t else ends
-        rows_ref[1, at + t * TILE : at + (t + 1) * TILE, :] = jnp.where(lane < HALF, tile, end)
+def unpack(packed, rows_ref, at):
+    row, lane = tile_iotas()
+    side = packed[MESSAGE - TILE :]
+    rows_ref[0, at : at + SIDE, :] = packed[:SIDE]
+    for t in range(6):
+        place = SIDE + (t % 3) * TILE
+        tile = turned(packed[place : place + TILE], HALF if t >= 3 else 0)
+        rows_ref[1, at + t * TILE : at + (t + 1) * TILE, :] = jnp.where(lane < HALF, tile, turned(side, HALF - t * TILE))
+    first = turned(side, -SIDE)
+    rows_ref[0, at + SIDE : at + STRIDE, :] = jnp.where((row >= 5) | (lane < 80), first, turned(side, 32, -2))
+    tail = jnp.where(row == 0, turned(first, 0, -4), turned(side, -88, -3))
+    rows_ref[1, at + SIDE : at + STRIDE, :] = jnp.where(lane < 40, tail, turned(side, -56, -2))
 
 
 def prepare_kernel(slab, chol_ref, rhs_ref):
@@ -123,7 +130,7 @@
 def work_kernel(slab, order, offsets, walk, arrived_ref, rhs_ref, body_ref, old_ref, send_ref, rows_ref, lhs_ref, table_ref):
     blocks = arrived_ref.shape[0]
     occupied, orbitals = body_ref.shape
-    rows, _ = packed_rows(occupied)
+    rows = STRIDE
     folds = send_ref.shape[0] // (blocks * walk)
     wide = folds * LANES
     at_energy, at_exponent, at_old, at_kinetic = offsets
@@ -134,7 +141,7 @@
     lane = lax.broadcasted_iota(jnp.int32, (GROUP, LANES), 1)
     for first in range(0, blocks, GROUP):
         for w in range(GROUP):
-            unpack(arrived_ref[order.index(first + w)].astype(F32), rows_ref, w * rows, occupied)
+            unpack(arrived_ref[order.index(first + w)].astype(F32), rows_ref, w * rows)
         for j in range(0, occupied, 2):
             for c, (low, high) in enumerate(chunks):
                 pair = [rows_ref[c, pl.ds(j + k, GROUP, stride=rows), :] for k in range(2)]
@@ -146,7 +153,7 @@
             mine = rows_ref[c, pl.ds(place, occupied), :][:, : high - low]
             here += jnp.sum(mine * body_ref[:, low:high], axis=(0, 1), keepdims=True)
         kinetic = jnp.where(own // GROUP == first // GROUP, here, kinetic)
-        parts = [rows_ref[0, pl.ds(occupied + k, GROUP, stride=rows), :] for k in range(3)]
+        parts = [rows_ref[0, pl.ds(rows - 3 + k, GROUP, stride=rows), :] for k in range(3)]
         noise.append((parts[0] + parts[1]) + parts[2])
         trace, total = tables_of(lhs_ref[...], rhs_ref, table_ref)
         force.append(jnp.where(lane < slab, trace, 0.0))
@@ -215,10 +222,9 @@
     order = exchange_order(blocks)
     vmem = pl.BlockSpec(memory_space=pltpu.VMEM)
     hbm = pl.BlockSpec(memory_space=pltpu.HBM)
-    first, second = packed_rows(occupied)
     pairs = occupied // 2
     small = pltpu.CompilerParams(vmem_limit_bytes=4 * 2**20)
-    message = (blocks, first + second, LANES)
+    message = (blocks, MESSAGE, LANES)
     packed = pl.pallas_call(
         functools.partial(pack_kernel, slab, order),
         out_shape=jax.ShapeDtypeStruct(message, BF16),
@@ -227,7 +233,7 @@
         scratch_shapes=[
             pltpu.VMEM(green_half.shape, BF16),
             pltpu.VMEM(field_noise.shape, F32),
-            pltpu.VMEM((first, LANES), F32),
+            pltpu.VMEM((2, STRIDE, LANES), F32),
             pltpu.VMEM(message, BF16),
             pltpu.SemaphoreType.DMA((2,)),
             pltpu.SemaphoreType.DMA((blocks,)),
@@ -252,7 +258,7 @@
         in_specs=[vmem] * 4,
         out_specs=vmem,
         scratch_shapes=[
-            pltpu.VMEM((round_up(orbitals, LANES) // LANES, GROUP * first, LANES), F32),
+            pltpu.VMEM((round_up(orbitals, LANES) // LANES, GROUP * STRIDE, LANES), F32),
             pltpu.VMEM((GROUP * occupied, orbitals), BF16),
             pltpu.VMEM((pairs, GROUP * occupied, 2 * LANES), F32),
         ],

time: 28.6 us -> 28.3 us (0.990)
  no operation moved by 1% of the time
where the time goes in v5:
time: 28.3 us; the launch traced here: 27.9 us
  blocking collectives  9.83 us (35%)
  starting transfers between devices  7.83 us (28%)
  Pallas kernels  4.38 us (15%)
  waiting for transfers between devices  3.02 us (11%)
  local copies, waits for them, and re-layouts  1.57 us (6%)
  between operations  1.31 us (5%)
    all_to_all x1, blocking collectives, on_device(): lax.all_to_all(send, ('blk', 'walk'), split_axis=0, concat_axis=0, tiled=...  9.83 us
    all_to_all x1, starting transfers between devices, on_device(): lax.all_to_all(packed, 'blk', split_axis=0, concat_axis=0, axis_index_gro...  7.83 us
    all_to_all x1, waiting for transfers between devices, on_device(): lax.all_to_all(packed, 'blk', split_axis=0, concat_axis=0, axis_index_gro...  3.02 us
    pallas_call x1, Pallas kernels, on_device(): pl.pallas_call(functools.partial(work_kernel, slab, order, offsets, walk)...  1.72 us
    pallas_call x1, Pallas kernels, on_device(): pl.pallas_call(functools.partial(pack_kernel, slab, order), out_shape=jax...  1.61 us
    unnamed x4, local copies, waits for them, and re-layouts  1.57 us
    pallas_call x1, Pallas kernels, on_device(): pl.pallas_call(functools.partial(finish_kernel, slab, offsets, blocks, wa...  0.89 us
  transfers between devices with their start and end apart: 1, of which 1 were waited for; matrix products, arithmetic and copies ran while one was open for 0% of the time, Pallas kernels for 1%

profile of v5, /device:TPU:0, one launch (start us, length us, event | category | flops | bytes accessed | tf_op | source)
XLA Modules:
  0.0 27.9 jit_solution(8370413297287932303)
XLA Ops:
  0.6 0.0 copy-start.1
  0.6 1.6 %pack.1 = bf16[8,80,128]{2,1,0:T(8,128)(2,1)} custom-call(bf16[1,50,200]{2,1,0:T(8,128)(2,1)} %green_hbm.1, f32[1,600]{1,0:T(1,128)} %noise_hbm.1), custom_call_target="tpu_custom_call" | custom-call | tf_op jit(solution)/shard_map/pack/pallas_call | solution.py:228
  2.3 7.8 %all-to-all-start = ((bf16[8,80,128]{2,1,0:T(8,128)(2,1)}), bf16[8,80,128]{2,1,0:T(8,128)(2,1)S(1)}, u32[]{:S(2)}, u32[]{:S(2)}) async-start(bf16[8,80,128]{2,1,0:T(8,128)(2,1)} %pack.1), calls=%async_computation | async-start | bytes 327680 | tf_op jit(solution)/shard_map/all_to_all | solution.py:244
  10.7 0.0 copy-start
  10.7 1.6 %copy-done = bf16[75,50,200]{2,0,1:T(8,128)(2,1)S(1)} copy-done((bf16[75,50,200]{2,0,1:T(8,128)(2,1)S(1)}, bf16[75,50,200]{2,0,1:T(8,128)(2,1)}, u32[]{:S(2)}) %copy-start) | copy-done | bytes 1500024
  12.3 0.2 prepare.1.rhs_ref
  12.5 3.0 %all-to-all-done.arrived_ref = bf16[8,80,128]{2,1,0:T(8,128)(2,1)S(1)} async-done(((bf16[8,80,128]{2,1,0:T(8,128)(2,1)}), bf16[8,80,128]{2,1,0:T(8,128)(2,1)S(1)}, u32[]{:S(2)}, u32[]{:S(2)}) %all-to-all-start) | async-done | bytes 163872 | tf_op jit(solution)/shard_map/all_to_all | solution.py:244
  15.5 0.0 copy-done.1
  15.5 1.7 %work.1 = f32[32,128]{1,0:T(8,128)S(1)} custom-call(bf16[8,80,128]{2,1,0:T(8,128)(2,1)S(1)} %all-to-all-done.arrived_ref, bf16[25,256,200]{2,1,0:T(8,128)(2,1)S(1)} %prepare.1.rhs_ref, f32[50,200]{1,0:T(8,128)S(1)} %copy-done.1, f32[1,1]{1,0:T(1,128)} %bitcast.9.old_ref), custom_call_target="tpu_custom_call" | custom-call | tf_op jit(solution)/shard_map/work/pallas_call | solution.py:255
  17.2 9.8 %all_to_all.16 = f32[32,1,128]{2,1,0:T(1,128)S(1)} all-to-all(f32[32,1,128]{2,1,0:T(1,128)S(1)} %bitcast.11), channel_id=1, replica_groups=mesh['blk'=8,'walk'=4] {'blk','walk'}, dimensions={0} | all-to-all | bytes 32768 | tf_op jit(solution)/shard_map/all_to_all | solution.py:268
  27.0 0.9 %finish.1 = (f32[1,600]{1,0:T(1,128)}, f32[1,1]{1,0:T(1,128)}, f32[1,1]{1,0:T(1,128)}, f32[1,1]{1,0:T(1,128)}) custom-call(f32[32,128]{1,0:T(8,128)S(1)} %bitcast.12), custom_call_target="tpu_custom_call" | custom-call | tf_op jit(solution)/shard_map/finish/pallas_call | solution.py:270
Async XLA Ops:
  0.6 14.9 %copy-start.1 = (f32[50,200]{1,0:T(8,128)S(1)}, f32[50,200]{1,0:T(8,128)}, u32[]{:S(2)}) copy-start(f32[50,200]{1,0:T(8,128)} %body_ref.1) | copy-start | bytes 120004
  2.3 13.2 %all-to-all-start = ((bf16[8,80,128]{2,1,0:T(8,128)(2,1)}), bf16[8,80,128]{2,1,0:T(8,128)(2,1)S(1)}, u32[]{:S(2)}, u32[]{:S(2)}) async-start(bf16[8,80,128]{2,1,0:T(8,128)(2,1)} %pack.1), calls=%async_computation | async-start | bytes 327680 | tf_op jit(solution)/shard_map/all_to_all | solution.py:244
  10.7 1.6 %copy-start = (bf16[75,50,200]{2,0,1:T(8,128)(2,1)S(1)}, bf16[75,50,200]{2,0,1:T(8,128)(2,1)}, u32[]{:S(2)}) copy-start(bf16[75,50,200]{2,0,1:T(8,128)(2,1)} %param.6) | copy-start | bytes 4500004

commit v6 on v5

--- a/solution.py
+++ b/solution.py
@@ -12,6 +12,7 @@
 LANES = 128
 TILE = 8
 HALF = LANES // 2
+SLOT = LANES // TILE
 GROUP = 8
 
 
@@ -101,30 +102,89 @@
     rows_ref[1, at + SIDE : at + STRIDE, :] = jnp.where(lane < 40, tail, turned(side, -56, -2))
 
 
+def plan_of(occupied):
+    tiles = [("pair", p) for p in range(-(-occupied // 2))]
+    tiles += [("eight", e) for e in range(-(-occupied // TILE))]
+    tiles = tiles[::-1]
+    place = {tile: divmod(k, 2) for k, tile in enumerate(tiles)}
+    pairs = [place["pair", p] for p in range(-(-occupied // 2))]
+    eights = [place["eight", e] for e in range(-(-occupied // TILE))]
+    return pairs, eights, -(-len(tiles) // 2)
+
+
 def prepare_kernel(slab, chol_ref, rhs_ref):
-    for i in range(chol_ref.shape[0]):
-        rhs_ref[i // 2, (i % 2) * LANES : (i % 2) * LANES + slab, :] = chol_ref[i]
+    occupied = chol_ref.shape[0]
+    pairs, eights, products = plan_of(occupied)
+    for p, t in eights + [(products - 1, 1)]:
+        rhs_ref[p, t * LANES : (t + 1) * LANES, :] = jnp.zeros((LANES, rhs_ref.shape[2]), BF16)
+    for i in range(occupied):
+        p, t = pairs[i // 2]
+        start = t * LANES + i % 2 * HALF
+        rhs_ref[p, start : start + HALF, :] = chol_ref[i, :HALF, :]
+        p, t = eights[i // TILE]
+        start = t * LANES + i % TILE * SLOT
+        rhs_ref[p, start : start + slab - HALF, :] = chol_ref[i, HALF:, :]
 
 
 def tables_of(lhs, rhs_ref, table_ref):
-    trace = [jnp.zeros((GROUP, LANES), F32) for _ in range(2)]
-    twice = [jnp.zeros((GROUP, LANES), F32) for _ in range(4)]
-    once = jnp.zeros((GROUP, LANES), F32)
-    for p in range(rhs_ref.shape[0]):
+    occupied = lhs.shape[0] // GROUP
+    pairs, eights, products = plan_of(occupied)
+    _, lane = tile_iotas()
+    low = lane < HALF
+    zero = jnp.zeros((GROUP, LANES), F32)
+    at = {place: ("pair", k) for k, place in enumerate(pairs)} | {place: ("eight", k) for k, place in enumerate(eights)}
+
+    def tile(place, j):
+        if j >= occupied:
+            return zero
+        p, t = place
+        return table_ref[p, j * GROUP : (j + 1) * GROUP, t * LANES : (t + 1) * LANES]
+
+    def diagonals(tiles):
+        for d in (1, 2, 4):
+            keep = (lane // SLOT) & d == 0
+            tiles = [jnp.where(keep, tiles[r], tiles[(r + d) % TILE]) for r in range(TILE)]
+        return tiles
+
+    def products_of(mine, other):
+        return [mine[r] * turned(other[-r % TILE], -r * SLOT) for r in range(TILE)]
+
+    once, twice = [zero] * 2, [zero] * 4
+    trace, ends = [zero] * 2, zero
+    done = {"pair": [], "eight": []}
+    for p in range(products):
         table_ref[p] = lax.dot_general(lhs, rhs_ref[p], (((1,), (1,)), ((), ())), preferred_element_type=F32)
-        for q in range(p):
-            mine = table_ref[p, q * 2 * GROUP : (q + 1) * 2 * GROUP, :]
-            other = table_ref[q, p * 2 * GROUP : (p + 1) * 2 * GROUP, :]
-            twice[0] += mine[:GROUP, :LANES] * other[:GROUP, :LANES]
-            twice[1] += mine[:GROUP, LANES:] * other[GROUP:, :LANES]
-            twice[2] += mine[GROUP:, :LANES] * other[:GROUP, LANES:]
-            twice[3] += mine[GROUP:, LANES:] * other[GROUP:, LANES:]
-        both = table_ref[p, p * 2 * GROUP : (p + 1) * 2 * GROUP, :]
-        trace[0] += both[:GROUP, :LANES]
-        trace[1] += both[GROUP:, LANES:]
-        once += both[:GROUP, :LANES] * both[:GROUP, :LANES] + both[GROUP:, LANES:] * both[GROUP:, LANES:]
-        twice[0] += both[:GROUP, LANES:] * both[GROUP:, :LANES]
-    return trace[0] + trace[1], once + 2.0 * ((twice[0] + twice[1]) + (twice[2] + twice[3]))
+        for t in range(2):
+            kind, k = at.get((p, t), (None, 0))
+            if kind == "pair":
+                for q in done[kind]:
+                    mine = [tile(pairs[k], 2 * q), tile(pairs[k], 2 * q + 1)]
+                    other = [tile(pairs[q], 2 * k), tile(pairs[q], 2 * k + 1)]
+                    twice[0] += jnp.where(low, mine[0], mine[1]) * jnp.where(low, other[0], other[1])
+                    twice[1] += jnp.where(low, mine[1], mine[0]) * turned(jnp.where(low, other[1], other[0]), HALF)
+                mine = [tile(pairs[k], 2 * k), tile(pairs[k], 2 * k + 1)]
+                both = jnp.where(low, mine[0], mine[1])
+                trace[k % 2] += both
+                once[0] += both * both
+                twice[2] += jnp.where(low, turned(mine[0], HALF) * mine[1], 0.0)
+                done[kind].append(k)
+            elif kind == "eight":
+                mine = diagonals([tile(eights[k], TILE * k + j) for j in range(TILE)])
+                ends += mine[0]
+                for product in products_of(mine, mine):
+                    once[1] += product
+                for q in done[kind]:
+                    mine = diagonals([tile(eights[k], TILE * q + j) for j in range(TILE)])
+                    other = diagonals([tile(eights[q], TILE * k + j) for j in range(TILE)])
+                    for product in products_of(mine, other):
+                        twice[3] += product
+                done[kind].append(k)
+    trace = trace[0] + trace[1]
+    trace = trace + turned(trace, HALF)
+    for lanes in (HALF, HALF // 2, HALF // 4):
+        ends = ends + turned(ends, lanes)
+    total = once[0] + once[1] + 2.0 * ((twice[0] + twice[1]) + (twice[2] + twice[3]))
+    return jnp.where(low, trace, ends), total
 
 
 def work_kernel(slab, order, offsets, walk, arrived_ref, rhs_ref, body_ref, old_ref, send_ref, rows_ref, lhs_ref, table_ref):
@@ -157,7 +217,7 @@
         noise.append((parts[0] + parts[1]) + parts[2])
         trace, total = tables_of(lhs_ref[...], rhs_ref, table_ref)
         force.append(jnp.where(lane < slab, trace, 0.0))
-        cross.append(jnp.where(lane < slab, total, 0.0))
+        cross.append(total)
     force = jnp.concatenate(force, axis=0)
     cross = jnp.concatenate(cross, axis=0)
     noise = jnp.concatenate(noise, axis=0)
@@ -222,7 +282,7 @@
     order = exchange_order(blocks)
     vmem = pl.BlockSpec(memory_space=pltpu.VMEM)
     hbm = pl.BlockSpec(memory_space=pltpu.HBM)
-    pairs = occupied // 2
+    products = plan_of(occupied)[2]
     small = pltpu.CompilerParams(vmem_limit_bytes=4 * 2**20)
     message = (blocks, MESSAGE, LANES)
     packed = pl.pallas_call(
@@ -244,7 +304,7 @@
     arrived = lax.all_to_all(packed, "blk", split_axis=0, concat_axis=0, axis_index_groups=[order], tiled=True)
     rhs = pl.pallas_call(
         functools.partial(prepare_kernel, slab),
-        out_shape=jax.ShapeDtypeStruct((pairs, 2 * LANES, orbitals), BF16),
+        out_shape=jax.ShapeDtypeStruct((products, 2 * LANES, orbitals), BF16),
         in_specs=[vmem],
         out_specs=vmem,
         compiler_params=pltpu.CompilerParams(vmem_limit_bytes=12 * 2**20),
@@ -260,7 +320,7 @@
         scratch_shapes=[
             pltpu.VMEM((round_up(orbitals, LANES) // LANES, GROUP * STRIDE, LANES), F32),
             pltpu.VMEM((GROUP * occupied, orbitals), BF16),
-            pltpu.VMEM((pairs, GROUP * occupied, 2 * LANES), F32),
+            pltpu.VMEM((products, GROUP * occupied, 2 * LANES), F32),
         ],
         compiler_params=pltpu.CompilerParams(vmem_limit_bytes=32 * 2**20),
         name="work",

time: 28.3 us -> 28.1 us (level)
  Pallas kernels: 4.38 us -> 3.98 us
    pallas_call x1, Pallas kernels: 1.72 us -> 1.31 us  [on_device(): pl.pallas_call(functools.partial(work_kernel, slab, order, offsets, walk)...]
where the time goes in v6:
time: 28.1 us; the launch traced here: 27.7 us
  blocking collectives  9.86 us (35%)
  starting transfers between devices  7.96 us (28%)
  Pallas kernels  3.98 us (14%)
  waiting for transfers between devices  2.99 us (11%)
  local copies, waits for them, and re-layouts  1.58 us (6%)
  between operations  1.31 us (5%)
    all_to_all x1, blocking collectives, on_device(): lax.all_to_all(send, ('blk', 'walk'), split_axis=0, concat_axis=0, tiled=...  9.86 us
    all_to_all x1, starting transfers between devices, on_device(): lax.all_to_all(packed, 'blk', split_axis=0, concat_axis=0, axis_index_gro...  7.96 us
    all_to_all x1, waiting for transfers between devices, on_device(): lax.all_to_all(packed, 'blk', split_axis=0, concat_axis=0, axis_index_gro...  2.99 us
    pallas_call x1, Pallas kernels, on_device(): pl.pallas_call(functools.partial(pack_kernel, slab, order), out_shape=jax...  1.59 us
    unnamed x4, local copies, waits for them, and re-layouts  1.58 us
    pallas_call x1, Pallas kernels, on_device(): pl.pallas_call(functools.partial(work_kernel, slab, order, offsets, walk)...  1.31 us
    pallas_call x1, Pallas kernels, on_device(): pl.pallas_call(functools.partial(finish_kernel, slab, offsets, blocks, wa...  0.89 us
  transfers between devices with their start and end apart: 1, of which 1 were waited for; matrix products, arithmetic and copies ran while one was open for 0% of the time, Pallas kernels for 1%

profile of v6, /device:TPU:0, one launch (start us, length us, event | category | flops | bytes accessed | tf_op | source)
XLA Modules:
  0.0 27.7 jit_solution(13029931742120912792)
XLA Ops:
  0.6 1.6 %pack.1 = bf16[8,80,128]{2,1,0:T(8,128)(2,1)} custom-call(bf16[1,50,200]{2,1,0:T(8,128)(2,1)} %green_hbm.1, f32[1,600]{1,0:T(1,128)} %noise_hbm.1), custom_call_target="tpu_custom_call" | custom-call | tf_op jit(solution)/shard_map/pack/pallas_call | solution.py:288
  2.2 0.0 copy-start.1
  2.2 8.0 %all-to-all-start = ((bf16[8,80,128]{2,1,0:T(8,128)(2,1)}), bf16[8,80,128]{2,1,0:T(8,128)(2,1)S(1)}, u32[]{:S(2)}, u32[]{:S(2)}) async-start(bf16[8,80,128]{2,1,0:T(8,128)(2,1)} %pack.1), calls=%async_computation | async-start | bytes 327680 | tf_op jit(solution)/shard_map/all_to_all | solution.py:304
  10.9 0.0 copy-start
  10.9 1.6 %copy-done = bf16[75,50,200]{2,0,1:T(8,128)(2,1)S(1)} copy-done((bf16[75,50,200]{2,0,1:T(8,128)(2,1)S(1)}, bf16[75,50,200]{2,0,1:T(8,128)(2,1)}, u32[]{:S(2)}) %copy-start) | copy-done | bytes 1500024
  12.4 0.2 prepare.1.rhs_ref
  12.6 3.0 %all-to-all-done.arrived_ref = bf16[8,80,128]{2,1,0:T(8,128)(2,1)S(1)} async-done(((bf16[8,80,128]{2,1,0:T(8,128)(2,1)}), bf16[8,80,128]{2,1,0:T(8,128)(2,1)S(1)}, u32[]{:S(2)}, u32[]{:S(2)}) %all-to-all-start) | async-done | bytes 163872 | tf_op jit(solution)/shard_map/all_to_all | solution.py:304
  15.6 0.0 copy-done.1
  15.6 1.3 %work.1 = f32[32,128]{1,0:T(8,128)S(1)} custom-call(bf16[8,80,128]{2,1,0:T(8,128)(2,1)S(1)} %all-to-all-done.arrived_ref, bf16[16,256,200]{2,1,0:T(8,128)(2,1)S(1)} %prepare.1.rhs_ref, f32[50,200]{1,0:T(8,128)S(1)} %copy-done.1, f32[1,1]{1,0:T(1,128)} %bitcast.9.old_ref), custom_call_target="tpu_custom_call" | custom-call | tf_op jit(solution)/shard_map/work/pallas_call | solution.py:315
  16.9 9.9 %all_to_all.16 = f32[32,1,128]{2,1,0:T(1,128)S(1)} all-to-all(f32[32,1,128]{2,1,0:T(1,128)S(1)} %bitcast.11), channel_id=1, replica_groups=mesh['blk'=8,'walk'=4] {'blk','walk'}, dimensions={0} | all-to-all | bytes 32768 | tf_op jit(solution)/shard_map/all_to_all | solution.py:328
  26.8 0.9 %finish.1 = (f32[1,600]{1,0:T(1,128)}, f32[1,1]{1,0:T(1,128)}, f32[1,1]{1,0:T(1,128)}, f32[1,1]{1,0:T(1,128)}) custom-call(f32[32,128]{1,0:T(8,128)S(1)} %bitcast.12), custom_call_target="tpu_custom_call" | custom-call | tf_op jit(solution)/shard_map/finish/pallas_call | solution.py:330
Async XLA Ops:
  2.2 13.4 %copy-start.1 = (f32[50,200]{1,0:T(8,128)S(1)}, f32[50,200]{1,0:T(8,128)}, u32[]{:S(2)}) copy-start(f32[50,200]{1,0:T(8,128)} %body_ref.1) | copy-start | bytes 120004
  2.2 13.4 %all-to-all-start = ((bf16[8,80,128]{2,1,0:T(8,128)(2,1)}), bf16[8,80,128]{2,1,0:T(8,128)(2,1)S(1)}, u32[]{:S(2)}, u32[]{:S(2)}) async-start(bf16[8,80,128]{2,1,0:T(8,128)(2,1)} %pack.1), calls=%async_computation | async-start | bytes 327680 | tf_op jit(solution)/shard_map/all_to_all | solution.py:304
  10.9 1.6 %copy-start = (bf16[75,50,200]{2,0,1:T(8,128)(2,1)S(1)}, bf16[75,50,200]{2,0,1:T(8,128)(2,1)}, u32[]{:S(2)}) copy-start(bf16[75,50,200]{2,0,1:T(8,128)(2,1)} %param.6) | copy-start | bytes 4500004

commit v7 on v6

--- a/solution.py
+++ b/solution.py
@@ -29,10 +29,10 @@
 
 
 def exchange_order(blocks):
-    if blocks % 4:
+    if blocks % 2:
         return list(range(blocks))
-    half = blocks // 4
-    return [2 * z + x for low in range(half - 1, -1, -1) for x in (1, 0) for z in (low, low + half)]
+    half = blocks // 2
+    return [block for low in [half - 1, *range(half - 1)] for block in (low, low + half)]
 
 
 MESSAGE = 80
@@ -50,7 +50,7 @@
     return pltpu.roll(tile, rows % TILE, 0) if rows % TILE else tile
 
 
-def pack_kernel(slab, order, green_hbm, noise_hbm, packed_hbm, green_ref, noise_ref, wide_ref, packed_ref, in_sems, out_sems):
+def pack_kernel(slab, order, green_hbm, noise_hbm, packed_hbm, green_ref, noise_ref, wide_ref, packed_ref, in_sems, out_sem):
     occupied, orbitals = green_ref.shape[1:]
     copies = [
         pltpu.make_async_copy(green_hbm, green_ref, in_sems.at[0]),
@@ -74,7 +74,6 @@
         side = jnp.where((lane >= t * TILE) & (lane < (t + 1) * TILE), turned(rest[t], t * TILE - HALF), side)
     whole = wide_ref[0, :SIDE, :]
     noise = noise_ref[...]
-    sends = []
     for slot, block in enumerate(order):
         piece = noise[:, block * slab : (block + 1) * slab]
         piece = jnp.concatenate([jnp.zeros((1, SIDE), F32), piece, jnp.zeros((1, LANES - SIDE - slab), F32)], axis=1)
@@ -82,10 +81,9 @@
         for k, part in enumerate(split_three(piece)):
             final = jnp.where((row == 5 + k) & (lane >= SIDE), part.astype(F32), final)
         packed_ref[slot] = jnp.concatenate([whole, *folded, final], axis=0).astype(BF16)
-        sends.append(pltpu.make_async_copy(packed_ref.at[slot], packed_hbm.at[slot], out_sems.at[slot]))
-        sends[-1].start()
-    for send in sends:
-        send.wait()
+    send = pltpu.make_async_copy(packed_ref, packed_hbm, out_sem)
+    send.start()
+    send.wait()
 
 
 def unpack(packed, rows_ref, at):
@@ -296,7 +294,7 @@
             pltpu.VMEM((2, STRIDE, LANES), F32),
             pltpu.VMEM(message, BF16),
             pltpu.SemaphoreType.DMA((2,)),
-            pltpu.SemaphoreType.DMA((blocks,)),
+            pltpu.SemaphoreType.DMA,
         ],
         compiler_params=pltpu.CompilerParams(vmem_limit_bytes=60 * 2**20),
         name="pack",

time: 28.1 us -> 27.9 us (level)
  no operation moved by 1% of the time
where the time goes in v7:
time: 27.9 us; the launch traced here: 27.5 us
  blocking collectives  9.97 us (36%)
  starting transfers between devices  7.96 us (29%)
  Pallas kernels  3.92 us (14%)
  waiting for transfers between devices  2.79 us (10%)
  local copies, waits for them, and re-layouts  1.58 us (6%)
  between operations  1.31 us (5%)
    all_to_all x1, blocking collectives, on_device(): lax.all_to_all(send, ('blk', 'walk'), split_axis=0, concat_axis=0, tiled=...  9.97 us
    all_to_all x1, starting transfers between devices, on_device(): lax.all_to_all(packed, 'blk', split_axis=0, concat_axis=0, axis_index_gro...  7.96 us
    all_to_all x1, waiting for transfers between devices, on_device(): lax.all_to_all(packed, 'blk', split_axis=0, concat_axis=0, axis_index_gro...  2.79 us
    unnamed x4, local copies, waits for them, and re-layouts  1.58 us
    pallas_call x1, Pallas kernels, on_device(): pl.pallas_call(functools.partial(pack_kernel, slab, order), out_shape=jax...  1.53 us
    pallas_call x1, Pallas kernels, on_device(): pl.pallas_call(functools.partial(work_kernel, slab, order, offsets, walk)...  1.32 us
    pallas_call x1, Pallas kernels, on_device(): pl.pallas_call(functools.partial(finish_kernel, slab, offsets, blocks, wa...  0.89 us
  transfers between devices with their start and end apart: 1, of which 1 were waited for; matrix products, arithmetic and copies ran while one was open for 0% of the time, Pallas kernels for 1%

profile of v7, /device:TPU:0, one launch (start us, length us, event | category | flops | bytes accessed | tf_op | source)
XLA Modules:
  0.0 27.5 jit_solution(3235143846559008649)
XLA Ops:
  0.6 1.5 %pack.1 = bf16[8,80,128]{2,1,0:T(8,128)(2,1)} custom-call(bf16[1,50,200]{2,1,0:T(8,128)(2,1)} %green_hbm.1, f32[1,600]{1,0:T(1,128)} %noise_hbm.1), custom_call_target="tpu_custom_call" | custom-call | tf_op jit(solution)/shard_map/pack/pallas_call | solution.py:286
  2.2 0.0 copy-start.1
  2.2 8.0 %all-to-all-start = ((bf16[8,80,128]{2,1,0:T(8,128)(2,1)}), bf16[8,80,128]{2,1,0:T(8,128)(2,1)S(1)}, u32[]{:S(2)}, u32[]{:S(2)}) async-start(bf16[8,80,128]{2,1,0:T(8,128)(2,1)} %pack.1), calls=%async_computation | async-start | bytes 327680 | tf_op jit(solution)/shard_map/all_to_all | solution.py:302
  10.8 0.0 copy-start
  10.8 1.6 %copy-done = bf16[75,50,200]{2,0,1:T(8,128)(2,1)S(1)} copy-done((bf16[75,50,200]{2,0,1:T(8,128)(2,1)S(1)}, bf16[75,50,200]{2,0,1:T(8,128)(2,1)}, u32[]{:S(2)}) %copy-start) | copy-done | bytes 1500024
  12.4 0.2 prepare.1.rhs_ref
  12.5 2.8 %all-to-all-done.arrived_ref = bf16[8,80,128]{2,1,0:T(8,128)(2,1)S(1)} async-done(((bf16[8,80,128]{2,1,0:T(8,128)(2,1)}), bf16[8,80,128]{2,1,0:T(8,128)(2,1)S(1)}, u32[]{:S(2)}, u32[]{:S(2)}) %all-to-all-start) | async-done | bytes 163872 | tf_op jit(solution)/shard_map/all_to_all | solution.py:302
  15.3 0.0 copy-done.1
  15.3 1.3 %work.1 = f32[32,128]{1,0:T(8,128)S(1)} custom-call(bf16[8,80,128]{2,1,0:T(8,128)(2,1)S(1)} %all-to-all-done.arrived_ref, bf16[16,256,200]{2,1,0:T(8,128)(2,1)S(1)} %prepare.1.rhs_ref, f32[50,200]{1,0:T(8,128)S(1)} %copy-done.1, f32[1,1]{1,0:T(1,128)} %bitcast.9.old_ref), custom_call_target="tpu_custom_call" | custom-call | tf_op jit(solution)/shard_map/work/pallas_call | solution.py:313
  16.7 10.0 %all_to_all.16 = f32[32,1,128]{2,1,0:T(1,128)S(1)} all-to-all(f32[32,1,128]{2,1,0:T(1,128)S(1)} %bitcast.11), channel_id=1, replica_groups=mesh['blk'=8,'walk'=4] {'blk','walk'}, dimensions={0} | all-to-all | bytes 32768 | tf_op jit(solution)/shard_map/all_to_all | solution.py:326
  26.6 0.9 %finish.1 = (f32[1,600]{1,0:T(1,128)}, f32[1,1]{1,0:T(1,128)}, f32[1,1]{1,0:T(1,128)}, f32[1,1]{1,0:T(1,128)}) custom-call(f32[32,128]{1,0:T(8,128)S(1)} %bitcast.12), custom_call_target="tpu_custom_call" | custom-call | tf_op jit(solution)/shard_map/finish/pallas_call | solution.py:328
Async XLA Ops:
  2.2 13.2 %copy-start.1 = (f32[50,200]{1,0:T(8,128)S(1)}, f32[50,200]{1,0:T(8,128)}, u32[]{:S(2)}) copy-start(f32[50,200]{1,0:T(8,128)} %body_ref.1) | copy-start | bytes 120004
  2.2 13.2 %all-to-all-start = ((bf16[8,80,128]{2,1,0:T(8,128)(2,1)}), bf16[8,80,128]{2,1,0:T(8,128)(2,1)S(1)}, u32[]{:S(2)}, u32[]{:S(2)}) async-start(bf16[8,80,128]{2,1,0:T(8,128)(2,1)} %pack.1), calls=%async_computation | async-start | bytes 327680 | tf_op jit(solution)/shard_map/all_to_all | solution.py:302
  10.8 1.6 %copy-start = (bf16[75,50,200]{2,0,1:T(8,128)(2,1)S(1)}, bf16[75,50,200]{2,0,1:T(8,128)(2,1)}, u32[]{:S(2)}) copy-start(bf16[75,50,200]{2,0,1:T(8,128)(2,1)} %param.6) | copy-start | bytes 4500004

commit v8 on v7

--- a/solution.py
+++ b/solution.py
@@ -50,17 +50,9 @@
     return pltpu.roll(tile, rows % TILE, 0) if rows % TILE else tile
 
 
-def pack_kernel(slab, order, green_hbm, noise_hbm, packed_hbm, green_ref, noise_ref, wide_ref, packed_ref, in_sems, out_sem):
+def pack_kernel(slab, order, green_ref, noise_ref, packed_ref, wide_ref):
     occupied, orbitals = green_ref.shape[1:]
-    copies = [
-        pltpu.make_async_copy(green_hbm, green_ref, in_sems.at[0]),
-        pltpu.make_async_copy(noise_hbm, noise_ref, in_sems.at[1]),
-    ]
-    for copy in copies:
-        copy.start()
     wide_ref[...] = jnp.zeros_like(wide_ref)
-    for copy in copies:
-        copy.wait()
     wide_ref[0, :occupied, :] = green_ref[0, :, :LANES].astype(F32)
     wide_ref[1, :occupied, : orbitals - LANES] = green_ref[0, :, LANES:].astype(F32)
     rest = [wide_ref[1, t * TILE : (t + 1) * TILE, :] for t in range(STRIDE // TILE)]
@@ -81,9 +73,6 @@
         for k, part in enumerate(split_three(piece)):
             final = jnp.where((row == 5 + k) & (lane >= SIDE), part.astype(F32), final)
         packed_ref[slot] = jnp.concatenate([whole, *folded, final], axis=0).astype(BF16)
-    send = pltpu.make_async_copy(packed_ref, packed_hbm, out_sem)
-    send.start()
-    send.wait()
 
 
 def unpack(packed, rows_ref, at):
@@ -279,23 +268,15 @@
     walk = lax.axis_size("walk")
     order = exchange_order(blocks)
     vmem = pl.BlockSpec(memory_space=pltpu.VMEM)
-    hbm = pl.BlockSpec(memory_space=pltpu.HBM)
     products = plan_of(occupied)[2]
     small = pltpu.CompilerParams(vmem_limit_bytes=4 * 2**20)
     message = (blocks, MESSAGE, LANES)
     packed = pl.pallas_call(
         functools.partial(pack_kernel, slab, order),
         out_shape=jax.ShapeDtypeStruct(message, BF16),
-        in_specs=[hbm, hbm],
-        out_specs=hbm,
-        scratch_shapes=[
-            pltpu.VMEM(green_half.shape, BF16),
-            pltpu.VMEM(field_noise.shape, F32),
-            pltpu.VMEM((2, STRIDE, LANES), F32),
-            pltpu.VMEM(message, BF16),
-            pltpu.SemaphoreType.DMA((2,)),
-            pltpu.SemaphoreType.DMA,
-        ],
+        in_specs=[vmem, vmem],
+        out_specs=vmem,
+        scratch_shapes=[pltpu.VMEM((2, STRIDE, LANES), F32)],
         compiler_params=pltpu.CompilerParams(vmem_limit_bytes=60 * 2**20),
         name="pack",
     )(green_half, field_noise)

time: 27.9 us -> 27.9 us (level)
  no operation moved by 1% of the time
where the time goes in v8:
time: 27.9 us; the launch traced here: 27.5 us
  blocking collectives  9.97 us (36%)
  starting transfers between devices  7.94 us (28%)
  Pallas kernels  3.9 us (14%)
  waiting for transfers between devices  2.79 us (10%)
  local copies, waits for them, and re-layouts  1.57 us (6%)
  between operations  1.3 us (5%)
    all_to_all x1, blocking collectives, on_device(): lax.all_to_all(send, ('blk', 'walk'), split_axis=0, concat_axis=0, tiled=...  9.97 us
    all_to_all x1, starting transfers between devices, on_device(): lax.all_to_all(packed, 'blk', split_axis=0, concat_axis=0, axis_index_gro...  7.94 us
    all_to_all x1, waiting for transfers between devices, on_device(): lax.all_to_all(packed, 'blk', split_axis=0, concat_axis=0, axis_index_gro...  2.79 us
    unnamed x4, local copies, waits for them, and re-layouts  1.57 us
    pallas_call x1, Pallas kernels, on_device(): pl.pallas_call(functools.partial(pack_kernel, slab, order), out_shape=jax...  1.51 us
    pallas_call x1, Pallas kernels, on_device(): pl.pallas_call(functools.partial(work_kernel, slab, order, offsets, walk)...  1.32 us
    pallas_call x1, Pallas kernels, on_device(): pl.pallas_call(functools.partial(finish_kernel, slab, offsets, blocks, wa...  0.89 us
  transfers between devices with their start and end apart: 1, of which 1 were waited for; matrix products, arithmetic and copies ran while one was open for 0% of the time, Pallas kernels for 1%

profile of v8, /device:TPU:0, one launch (start us, length us, event | category | flops | bytes accessed | tf_op | source)
XLA Modules:
  0.0 27.5 jit_solution(14959726292496036422)
XLA Ops:
  0.6 1.5 %pack.1 = bf16[8,80,128]{2,1,0:T(8,128)(2,1)} custom-call(bf16[1,50,200]{2,1,0:T(8,128)(2,1)} %green_ref.1, f32[1,600]{1,0:T(1,128)} %noise_ref.1), custom_call_target="tpu_custom_call" | custom-call | tf_op jit(solution)/shard_map/pack/pallas_call | solution.py:274
  2.1 0.0 copy-start.1
  2.1 7.9 %all-to-all-start = ((bf16[8,80,128]{2,1,0:T(8,128)(2,1)}), bf16[8,80,128]{2,1,0:T(8,128)(2,1)S(1)}, u32[]{:S(2)}, u32[]{:S(2)}) async-start(bf16[8,80,128]{2,1,0:T(8,128)(2,1)} %pack.1), calls=%async_computation | async-start | bytes 327680 | tf_op jit(solution)/shard_map/all_to_all | solution.py:283
  10.7 0.0 copy-start
  10.8 1.6 %copy-done = bf16[75,50,200]{2,0,1:T(8,128)(2,1)S(1)} copy-done((bf16[75,50,200]{2,0,1:T(8,128)(2,1)S(1)}, bf16[75,50,200]{2,0,1:T(8,128)(2,1)}, u32[]{:S(2)}) %copy-start) | copy-done | bytes 1500024
  12.3 0.2 prepare.1.rhs_ref
  12.5 2.8 %all-to-all-done.arrived_ref = bf16[8,80,128]{2,1,0:T(8,128)(2,1)S(1)} async-done(((bf16[8,80,128]{2,1,0:T(8,128)(2,1)}), bf16[8,80,128]{2,1,0:T(8,128)(2,1)S(1)}, u32[]{:S(2)}, u32[]{:S(2)}) %all-to-all-start) | async-done | bytes 163872 | tf_op jit(solution)/shard_map/all_to_all | solution.py:283
  15.3 0.0 copy-done.1
  15.3 1.3 %work.1 = f32[32,128]{1,0:T(8,128)S(1)} custom-call(bf16[8,80,128]{2,1,0:T(8,128)(2,1)S(1)} %all-to-all-done.arrived_ref, bf16[16,256,200]{2,1,0:T(8,128)(2,1)S(1)} %prepare.1.rhs_ref, f32[50,200]{1,0:T(8,128)S(1)} %copy-done.1, f32[1,1]{1,0:T(1,128)} %bitcast.9.old_ref), custom_call_target="tpu_custom_call" | custom-call | tf_op jit(solution)/shard_map/work/pallas_call | solution.py:294
  16.6 10.0 %all_to_all.16 = f32[32,1,128]{2,1,0:T(1,128)S(1)} all-to-all(f32[32,1,128]{2,1,0:T(1,128)S(1)} %bitcast.11), channel_id=1, replica_groups=mesh['blk'=8,'walk'=4] {'blk','walk'}, dimensions={0} | all-to-all | bytes 32768 | tf_op jit(solution)/shard_map/all_to_all | solution.py:307
  26.6 0.9 %finish.1 = (f32[1,600]{1,0:T(1,128)}, f32[1,1]{1,0:T(1,128)}, f32[1,1]{1,0:T(1,128)}, f32[1,1]{1,0:T(1,128)}) custom-call(f32[32,128]{1,0:T(8,128)S(1)} %bitcast.12), custom_call_target="tpu_custom_call" | custom-call | tf_op jit(solution)/shard_map/finish/pallas_call | solution.py:309
Async XLA Ops:
  2.1 13.2 %copy-start.1 = (f32[50,200]{1,0:T(8,128)S(1)}, f32[50,200]{1,0:T(8,128)}, u32[]{:S(2)}) copy-start(f32[50,200]{1,0:T(8,128)} %body_ref.1) | copy-start | bytes 120004
  2.1 13.1 %all-to-all-start = ((bf16[8,80,128]{2,1,0:T(8,128)(2,1)}), bf16[8,80,128]{2,1,0:T(8,128)(2,1)S(1)}, u32[]{:S(2)}, u32[]{:S(2)}) async-start(bf16[8,80,128]{2,1,0:T(8,128)(2,1)} %pack.1), calls=%async_computation | async-start | bytes 327680 | tf_op jit(solution)/shard_map/all_to_all | solution.py:283
  10.7 1.6 %copy-start = (bf16[75,50,200]{2,0,1:T(8,128)(2,1)S(1)}, bf16[75,50,200]{2,0,1:T(8,128)(2,1)}, u32[]{:S(2)}) copy-start(bf16[75,50,200]{2,0,1:T(8,128)(2,1)} %param.6) | copy-start | bytes 4500004

commit v9 on v8

--- a/solution.py
+++ b/solution.py
@@ -64,7 +64,7 @@
     side = jnp.where(row == 4, jnp.where(lane < 88, turned(after, SIDE, 4), turned(after, 88, 3)), side)
     for t in range(6):
         side = jnp.where((lane >= t * TILE) & (lane < (t + 1) * TILE), turned(rest[t], t * TILE - HALF), side)
-    whole = wide_ref[0, :SIDE, :]
+    whole = green_ref[0, :SIDE, :LANES].astype(F32)
     noise = noise_ref[...]
     for slot, block in enumerate(order):
         piece = noise[:, block * slab : (block + 1) * slab]
@@ -246,11 +246,13 @@
     for b in range(blocks):
         force_ref[:, b * slab : (b + 1) * slab] = own[b : b + 1, :slab]
     sums = jnp.concatenate(sums, axis=0)
-    exponent = sums[:, at_exponent : at_exponent + blocks]
-    old = sums[:, at_old : at_old + blocks]
-    kinetic = sums[:, at_kinetic : at_kinetic + blocks]
-    weight = old * jnp.exp(exponent - 0.01 * kinetic)
-    index = lax.broadcasted_iota(jnp.int32, (walk, blocks), 1) * walk + lax.broadcasted_iota(jnp.int32, (walk, blocks), 0)
+    place = lax.broadcasted_iota(jnp.int32, (walk, wide), 1) - at_exponent
+    inside = (place >= 0) & (place < blocks)
+    old = pltpu.roll(sums, wide - (at_old - at_exponent), 1)
+    kinetic = pltpu.roll(sums, wide - (at_kinetic - at_exponent), 1)
+    change = jnp.where(inside, sums - 0.01 * kinetic, 0.0)
+    weight = jnp.where(inside, old * jnp.exp(change), 0.0)
+    index = place * walk + lax.broadcasted_iota(jnp.int32, (walk, wide), 0)
     rank = own_block * walk + own_walk
 
     def total(values):
@@ -258,7 +260,7 @@
 
     before = total(jnp.where(index < rank, weight, 0.0))
     weight_ref[...] = total(jnp.where(index == rank, weight, 0.0))
-    energy_ref[...] = total(jnp.where(lane == at_energy, own, 0.0)) + total(jnp.where(index == rank, kinetic, 0.0))
+    energy_ref[...] = total(jnp.where(lane == at_energy, own, 0.0)) + total(jnp.where(inside & (index == rank), kinetic, 0.0))
     comb_ref[...] = before * (blocks * walk) / total(weight) - rank.astype(F32)
 
 

time: 27.9 us -> 27.7 us (level)
  no operation moved by 1% of the time
where the time goes in v9:
time: 27.7 us; the launch traced here: 27.3 us
  blocking collectives  9.97 us (36%)
  starting transfers between devices  7.94 us (29%)
  Pallas kernels  3.77 us (14%)
  waiting for transfers between devices  2.79 us (10%)
  local copies, waits for them, and re-layouts  1.57 us (6%)
  between operations  1.3 us (5%)
    all_to_all x1, blocking collectives, on_device(): lax.all_to_all(send, ('blk', 'walk'), split_axis=0, concat_axis=0, tiled=...  9.97 us
    all_to_all x1, starting transfers between devices, on_device(): lax.all_to_all(packed, 'blk', split_axis=0, concat_axis=0, axis_index_gro...  7.94 us
    all_to_all x1, waiting for transfers between devices, on_device(): lax.all_to_all(packed, 'blk', split_axis=0, concat_axis=0, axis_index_gro...  2.79 us
    unnamed x4, local copies, waits for them, and re-layouts  1.57 us
    pallas_call x1, Pallas kernels, on_device(): pl.pallas_call(functools.partial(pack_kernel, slab, order), out_shape=jax...  1.51 us
    pallas_call x1, Pallas kernels, on_device(): pl.pallas_call(functools.partial(work_kernel, slab, order, offsets, walk)...  1.31 us
    pallas_call x1, Pallas kernels, on_device(): pl.pallas_call(functools.partial(finish_kernel, slab, offsets, blocks, wa...  0.77 us
  transfers between devices with their start and end apart: 1, of which 1 were waited for; matrix products, arithmetic and copies ran while one was open for 0% of the time, Pallas kernels for 1%

profile of v9, /device:TPU:0, one launch (start us, length us, event | category | flops | bytes accessed | tf_op | source)
XLA Modules:
  0.0 27.3 jit_solution(16979221453096071783)
XLA Ops:
  0.6 1.5 %pack.1 = bf16[8,80,128]{2,1,0:T(8,128)(2,1)} custom-call(bf16[1,50,200]{2,1,0:T(8,128)(2,1)} %green_ref.1, f32[1,600]{1,0:T(1,128)} %noise_ref.1), custom_call_target="tpu_custom_call" | custom-call | tf_op jit(solution)/shard_map/pack/pallas_call | solution.py:276
  2.1 0.0 copy-start.1
  2.1 7.9 %all-to-all-start = ((bf16[8,80,128]{2,1,0:T(8,128)(2,1)}), bf16[8,80,128]{2,1,0:T(8,128)(2,1)S(1)}, u32[]{:S(2)}, u32[]{:S(2)}) async-start(bf16[8,80,128]{2,1,0:T(8,128)(2,1)} %pack.1), calls=%async_computation | async-start | bytes 327680 | tf_op jit(solution)/shard_map/all_to_all | solution.py:285
  10.7 0.0 copy-start
  10.7 1.6 %copy-done = bf16[75,50,200]{2,0,1:T(8,128)(2,1)S(1)} copy-done((bf16[75,50,200]{2,0,1:T(8,128)(2,1)S(1)}, bf16[75,50,200]{2,0,1:T(8,128)(2,1)}, u32[]{:S(2)}) %copy-start) | copy-done | bytes 1500024
  12.3 0.2 prepare.1.rhs_ref
  12.5 2.8 %all-to-all-done.arrived_ref = bf16[8,80,128]{2,1,0:T(8,128)(2,1)S(1)} async-done(((bf16[8,80,128]{2,1,0:T(8,128)(2,1)}), bf16[8,80,128]{2,1,0:T(8,128)(2,1)S(1)}, u32[]{:S(2)}, u32[]{:S(2)}) %all-to-all-start) | async-done | bytes 163872 | tf_op jit(solution)/shard_map/all_to_all | solution.py:285
  15.3 0.0 copy-done.1
  15.3 1.3 %work.1 = f32[32,128]{1,0:T(8,128)S(1)} custom-call(bf16[8,80,128]{2,1,0:T(8,128)(2,1)S(1)} %all-to-all-done.arrived_ref, bf16[16,256,200]{2,1,0:T(8,128)(2,1)S(1)} %prepare.1.rhs_ref, f32[50,200]{1,0:T(8,128)S(1)} %copy-done.1, f32[1,1]{1,0:T(1,128)} %bitcast.9.old_ref), custom_call_target="tpu_custom_call" | custom-call | tf_op jit(solution)/shard_map/work/pallas_call | solution.py:296
  16.6 10.0 %all_to_all.16 = f32[32,1,128]{2,1,0:T(1,128)S(1)} all-to-all(f32[32,1,128]{2,1,0:T(1,128)S(1)} %bitcast.11), channel_id=1, replica_groups=mesh['blk'=8,'walk'=4] {'blk','walk'}, dimensions={0} | all-to-all | bytes 32768 | tf_op jit(solution)/shard_map/all_to_all | solution.py:309
  26.6 0.8 %finish.1 = (f32[1,600]{1,0:T(1,128)}, f32[1,1]{1,0:T(1,128)}, f32[1,1]{1,0:T(1,128)}, f32[1,1]{1,0:T(1,128)}) custom-call(f32[32,128]{1,0:T(8,128)S(1)} %bitcast.12), custom_call_target="tpu_custom_call" | custom-call | tf_op jit(solution)/shard_map/finish/pallas_call | solution.py:311
Async XLA Ops:
  2.1 13.2 %copy-start.1 = (f32[50,200]{1,0:T(8,128)S(1)}, f32[50,200]{1,0:T(8,128)}, u32[]{:S(2)}) copy-start(f32[50,200]{1,0:T(8,128)} %body_ref.1) | copy-start | bytes 120004
  2.1 13.1 %all-to-all-start = ((bf16[8,80,128]{2,1,0:T(8,128)(2,1)}), bf16[8,80,128]{2,1,0:T(8,128)(2,1)S(1)}, u32[]{:S(2)}, u32[]{:S(2)}) async-start(bf16[8,80,128]{2,1,0:T(8,128)(2,1)} %pack.1), calls=%async_computation | async-start | bytes 327680 | tf_op jit(solution)/shard_map/all_to_all | solution.py:285
  10.7 1.6 %copy-start = (bf16[75,50,200]{2,0,1:T(8,128)(2,1)S(1)}, bf16[75,50,200]{2,0,1:T(8,128)(2,1)}, u32[]{:S(2)}) copy-start(bf16[75,50,200]{2,0,1:T(8,128)(2,1)} %param.6) | copy-start | bytes 4500004

commit v10 on v9

--- a/solution.py
+++ b/solution.py
@@ -91,8 +91,8 @@
 
 def plan_of(occupied):
     tiles = [("pair", p) for p in range(-(-occupied // 2))]
-    tiles += [("eight", e) for e in range(-(-occupied // TILE))]
-    tiles = tiles[::-1]
+    middle = TILE + 1
+    tiles[middle:middle] = [("eight", e) for e in range(-(-occupied // TILE))]
     place = {tile: divmod(k, 2) for k, tile in enumerate(tiles)}
     pairs = [place["pair", p] for p in range(-(-occupied // 2))]
     eights = [place["eight", e] for e in range(-(-occupied // TILE))]

time: 27.7 us -> 27.7 us (level)
  no operation moved by 1% of the time
where the time goes in v10:
time: 27.7 us; the launch traced here: 27.4 us
  blocking collectives  9.94 us (36%)
  starting transfers between devices  7.94 us (29%)
  Pallas kernels  3.8 us (14%)
  waiting for transfers between devices  2.79 us (10%)
  local copies, waits for them, and re-layouts  1.57 us (6%)
  between operations  1.3 us (5%)
    all_to_all x1, blocking collectives, on_device(): lax.all_to_all(send, ('blk', 'walk'), split_axis=0, concat_axis=0, tiled=...  9.94 us
    all_to_all x1, starting transfers between devices, on_device(): lax.all_to_all(packed, 'blk', split_axis=0, concat_axis=0, axis_index_gro...  7.94 us
    all_to_all x1, waiting for transfers between devices, on_device(): lax.all_to_all(packed, 'blk', split_axis=0, concat_axis=0, axis_index_gro...  2.79 us
    unnamed x4, local copies, waits for them, and re-layouts  1.57 us
    pallas_call x1, Pallas kernels, on_device(): pl.pallas_call(functools.partial(pack_kernel, slab, order), out_shape=jax...  1.51 us
    pallas_call x1, Pallas kernels, on_device(): pl.pallas_call(functools.partial(work_kernel, slab, order, offsets, walk)...  1.35 us
    pallas_call x1, Pallas kernels, on_device(): pl.pallas_call(functools.partial(finish_kernel, slab, offsets, blocks, wa...  0.77 us
  transfers between devices with their start and end apart: 1, of which 1 were waited for; matrix products, arithmetic and copies ran while one was open for 0% of the time, Pallas kernels for 1%

profile of v10, /device:TPU:0, one launch (start us, length us, event | category | flops | bytes accessed | tf_op | source)
XLA Modules:
  0.0 27.4 jit_solution(14128526754042387244)
XLA Ops:
  0.6 1.5 %pack.1 = bf16[8,80,128]{2,1,0:T(8,128)(2,1)} custom-call(bf16[1,50,200]{2,1,0:T(8,128)(2,1)} %green_ref.1, f32[1,600]{1,0:T(1,128)} %noise_ref.1), custom_call_target="tpu_custom_call" | custom-call | tf_op jit(solution)/shard_map/pack/pallas_call | solution.py:276
  2.1 0.0 copy-start.1
  2.1 7.9 %all-to-all-start = ((bf16[8,80,128]{2,1,0:T(8,128)(2,1)}), bf16[8,80,128]{2,1,0:T(8,128)(2,1)S(1)}, u32[]{:S(2)}, u32[]{:S(2)}) async-start(bf16[8,80,128]{2,1,0:T(8,128)(2,1)} %pack.1), calls=%async_computation | async-start | bytes 327680 | tf_op jit(solution)/shard_map/all_to_all | solution.py:285
  10.7 0.0 copy-start
  10.7 1.6 %copy-done = bf16[75,50,200]{2,0,1:T(8,128)(2,1)S(1)} copy-done((bf16[75,50,200]{2,0,1:T(8,128)(2,1)S(1)}, bf16[75,50,200]{2,0,1:T(8,128)(2,1)}, u32[]{:S(2)}) %copy-start) | copy-done | bytes 1500024
  12.3 0.2 prepare.1.rhs_ref
  12.5 2.8 %all-to-all-done.arrived_ref = bf16[8,80,128]{2,1,0:T(8,128)(2,1)S(1)} async-done(((bf16[8,80,128]{2,1,0:T(8,128)(2,1)}), bf16[8,80,128]{2,1,0:T(8,128)(2,1)S(1)}, u32[]{:S(2)}, u32[]{:S(2)}) %all-to-all-start) | async-done | bytes 163872 | tf_op jit(solution)/shard_map/all_to_all | solution.py:285
  15.3 0.0 copy-done.1
  15.3 1.4 %work.1 = f32[32,128]{1,0:T(8,128)S(1)} custom-call(bf16[8,80,128]{2,1,0:T(8,128)(2,1)S(1)} %all-to-all-done.arrived_ref, bf16[16,256,200]{2,1,0:T(8,128)(2,1)S(1)} %prepare.1.rhs_ref, f32[50,200]{1,0:T(8,128)S(1)} %copy-done.1, f32[1,1]{1,0:T(1,128)} %bitcast.9.old_ref), custom_call_target="tpu_custom_call" | custom-call | tf_op jit(solution)/shard_map/work/pallas_call | solution.py:296
  16.6 9.9 %all_to_all.16 = f32[32,1,128]{2,1,0:T(1,128)S(1)} all-to-all(f32[32,1,128]{2,1,0:T(1,128)S(1)} %bitcast.11), channel_id=1, replica_groups=mesh['blk'=8,'walk'=4] {'blk','walk'}, dimensions={0} | all-to-all | bytes 32768 | tf_op jit(solution)/shard_map/all_to_all | solution.py:309
  26.6 0.8 %finish.1 = (f32[1,600]{1,0:T(1,128)}, f32[1,1]{1,0:T(1,128)}, f32[1,1]{1,0:T(1,128)}, f32[1,1]{1,0:T(1,128)}) custom-call(f32[32,128]{1,0:T(8,128)S(1)} %bitcast.12), custom_call_target="tpu_custom_call" | custom-call | tf_op jit(solution)/shard_map/finish/pallas_call | solution.py:311
Async XLA Ops:
  2.1 13.2 %copy-start.1 = (f32[50,200]{1,0:T(8,128)S(1)}, f32[50,200]{1,0:T(8,128)}, u32[]{:S(2)}) copy-start(f32[50,200]{1,0:T(8,128)} %body_ref.1) | copy-start | bytes 120004
  2.1 13.1 %all-to-all-start = ((bf16[8,80,128]{2,1,0:T(8,128)(2,1)}), bf16[8,80,128]{2,1,0:T(8,128)(2,1)S(1)}, u32[]{:S(2)}, u32[]{:S(2)}) async-start(bf16[8,80,128]{2,1,0:T(8,128)(2,1)} %pack.1), calls=%async_computation | async-start | bytes 327680 | tf_op jit(solution)/shard_map/all_to_all | solution.py:285
  10.7 1.6 %copy-start = (bf16[75,50,200]{2,0,1:T(8,128)(2,1)S(1)}, bf16[75,50,200]{2,0,1:T(8,128)(2,1)}, u32[]{:S(2)}) copy-start(bf16[75,50,200]{2,0,1:T(8,128)(2,1)} %param.6) | copy-start | bytes 4500004
